TPU v7x, 128 devices: a whole 4x4x4 slice. The times are simulated.
128 devices in a mesh: dom: 64 (over x, y, z_hi, core), feat: 2 (over z_lo).
Axes of the slice: x: 4, y: 4, z: 4 (z_hi: 2, z_lo: 2; z = z_hi * 2 + z_lo), core: 2. Of those that a mesh axis runs over, the one named last changes fastest.
Arguments:
- features: bfloat16 [65536, 128], P('dom', 'feat'), may hold values from -6 to 6
- weight: bfloat16 [128, 256], P('feat'), may hold values from -0.5 to 0.5
- stale_cache: bfloat16 [65536, 256], P(None, 'feat'), may hold values from -6 to 6
- adj_tiles: bfloat16 [49152, 128, 128], P('dom'), may hold values from -0.0546875 to 0.0546875
- tile_src: int32 [49152], P('dom'), may hold values from 0 to 511
- tile_dst: int32 [49152], P('dom'), may hold values from 0 to 7
- tile_count: int32 [64], P('dom'), may hold values from 153 to 768, as said below
- refresh: int32 [64, 256], replicated, may hold values from 0 to 1023, as said below
- train_mask: int32 [65536], P('dom'), may hold values 0 or 1
- grad_hidden: bfloat16 [65536, 256], P('dom', 'feat'), may hold values from -6 to 6
Outputs:
- hidden: bfloat16 [65536, 256], P('dom', 'feat')
- grad_features: bfloat16 [65536, 128], P('dom', 'feat')
- grad_weight: float32 [128, 256], P('feat')
Inputs may be any that keep to these rules, and one draw needn't show every extreme that they name: `tile_count`: some partition has all 768 slots live. `refresh`: the 256 entries of one partition are distinct.
All inputs are finite; a program needn't handle non-finite values. No bound on the sum of `train_mask` on one device may be relied on, other than what follows from the above.
Results may differ from a plain program's by a relative error of at most 0.027.
Values may be sent and summed in bfloat16 or wider, within the bound.
A program may use at most 256 MiB of HBM per device.

v0:
```python
import math

import jax
import jax.numpy as jnp
from jax import lax
from jax.sharding import PartitionSpec as P


def shards(
    features,
    weight,
    stale_cache,
    adj_tiles,
    tile_src,
    tile_dst,
    tile_count,
    refresh,
    train_mask,
    grad_hidden,
):
    highest = lax.Precision.HIGHEST
    row_count = features.shape[0]
    tile_size = adj_tiles.shape[1]
    tile_slots = adj_tiles.shape[0]
    width = grad_hidden.shape[1]
    per_part = row_count // tile_size
    owner_id = lax.axis_index("dom")
    part_count = lax.axis_size("dom")
    own_start = owner_id * row_count
    partial_rows = jnp.dot(features, weight, preferred_element_type=jnp.float32)
    fresh_rows = lax.psum_scatter(partial_rows, "feat", scatter_dimension=1, tiled=True).astype(
        jnp.bfloat16
    )
    own_list = lax.dynamic_index_in_dim(refresh, owner_id, 0, keepdims=False)
    offsets = jnp.arange(part_count, dtype=jnp.int32)[:, None] * row_count
    global_rows = (offsets + refresh).reshape(-1)
    picked = fresh_rows[own_list]
    arrived = lax.all_gather(picked, "dom", axis=0, tiled=True)
    source = stale_cache.at[global_rows].set(arrived)
    source = lax.dynamic_update_slice_in_dim(source, fresh_rows, own_start, 0)
    source_blocks = source.reshape(-1, tile_size, width)
    live_count = tile_count[0]
    group_size = math.gcd(32, tile_slots)
    trips = (live_count + group_size - 1) // group_size
    group_ids = jnp.arange(group_size, dtype=jnp.int32)
    local_blocks = jnp.arange(per_part, dtype=jnp.int32)

    def take_group(index):
        first_slot = index * group_size
        tiles_now = lax.dynamic_slice_in_dim(adj_tiles, first_slot, group_size, 0)
        src_now = lax.dynamic_slice_in_dim(tile_src, first_slot, group_size, 0)
        dst_now = lax.dynamic_slice_in_dim(tile_dst, first_slot, group_size, 0)
        live_mask = (first_slot + group_ids < live_count).astype(jnp.float32)
        return (tiles_now, src_now, dst_now, live_mask)

    def forward_step(index, totals):
        tiles_now, src_now, dst_now, live_mask = take_group(index)
        product = jnp.einsum(
            "tij,tjc->tic", tiles_now, source_blocks[src_now], preferred_element_type=jnp.float32
        )
        onehot = (dst_now[:, None] == local_blocks[None, :]).astype(jnp.float32) * live_mask[
            :, None
        ]
        return totals + jnp.einsum("tb,tic->bic", onehot, product, precision=highest)

    totals = lax.fori_loop(
        0, trips, forward_step, jnp.zeros((per_part, tile_size, width), jnp.float32)
    )
    pre_act = totals.reshape(row_count, width)
    hidden = jnp.maximum(pre_act, 0.0).astype(jnp.bfloat16)
    pass_mask = train_mask.astype(jnp.float32)[:, None] * (pre_act > 0).astype(jnp.float32)
    delta_rows = (grad_hidden.astype(jnp.float32) * pass_mask).astype(jnp.bfloat16)
    delta_blocks = delta_rows.reshape(per_part, tile_size, width)

    def backward_step(index, buffer):
        tiles_now, src_now, dst_now, live_mask = take_group(index)
        contrib = jnp.einsum(
            "tji,tjc->tic", tiles_now, delta_blocks[dst_now], preferred_element_type=jnp.float32
        )
        return buffer.at[src_now].add(contrib * live_mask[:, None, None])

    buffer = lax.fori_loop(
        0, trips, backward_step, jnp.zeros((part_count * per_part, tile_size, width), jnp.float32)
    )
    flat_grads = buffer.reshape(-1, width)
    own_grad = lax.dynamic_slice_in_dim(flat_grads, own_start, row_count, 0)
    keep_mask = (jnp.arange(part_count, dtype=jnp.int32) != owner_id).astype(jnp.float32)
    remote_terms = flat_grads[global_rows].reshape(part_count, -1, width) * keep_mask[:, None, None]
    carried = lax.psum_scatter(
        remote_terms.reshape(-1, width), "dom", scatter_dimension=0, tiled=True
    )
    grad_fresh = own_grad.at[own_list].add(carried).astype(jnp.bfloat16)
    all_grad = lax.all_gather(grad_fresh, "feat", axis=1, tiled=True)
    grad_features = lax.dot_general(
        all_grad, weight, (((1,), (1,)), ((), ())), preferred_element_type=jnp.float32
    ).astype(jnp.bfloat16)
    local_weight = lax.dot_general(
        features, all_grad, (((0,), (0,)), ((), ())), preferred_element_type=jnp.float32
    )
    grad_weight = lax.psum(local_weight, "dom")
    return (hidden, grad_features, grad_weight)


def solution(mesh):
    placed = (
        P("dom", "feat"),
        P("feat", None),
        P(None, "feat"),
        P("dom", None, None),
        P("dom"),
        P("dom"),
        P("dom"),
        P(),
        P("dom"),
        P("dom", "feat"),
    )
    return jax.shard_map(
        shards,
        mesh=mesh,
        in_specs=placed,
        out_specs=(P("dom", "feat"), P("dom", "feat"), P("feat", None)),
        check_vma=False,
    )
```

profile of v0, /device:TPU:0, one launch (start us, length us, event | category | flops | bytes accessed | tf_op | source)
XLA Modules:
  0.0 1743.7 jit_solution(13621818902180389100)
XLA Ops:
  7.3 13.7 copy.50
  22.4 25.4 %reduce-scatter.3.cloned.1.call-done = f32[1024,128]{1,0:T(8,128)} async-done(((f32[1024,256]{1,0:T(8,128)}), f32[1024,128]{1,0:T(8,128)}) %reduce-scatter.3.cloned.1.call-update) | async-done | bytes 524304 | tf_op jit(solution)/shard_map/reduce_scatter | solution.py:31
  52.8 73.5 %all-gather.3.cloned.1.call-done = bf16[16384,128]{1,0:T(8,128)(2,1)} async-done(((bf16[256,128]{1,0:T(8,128)(2,1)}), bf16[16384,128]{1,0:T(8,128)(2,1)}) %all-gather.3.cloned.1.call-update) | async-done | bytes 4194320 | tf_op jit(solution)/shard_map/all_gather | solution.py:38
  126.3 56.4 %scatter_fusion.1 = bf16[65536,128]{1,0:T(8,128)(2,1)} fusion(bf16[65536,128]{1,0:T(8,128)(2,1)} %copy.50, s32[16384]{0:T(1024)S(1)} %bitcast.44, bf16[16384,128]{1,0:T(8,128)(2,1)} %all-gather.3.cloned.1.call-done), kind=kCustom, calls=%fused_computation.5 | custom fusion | bytes 12648448 | tf_op jit(solution)/shard_map/scatter | solution.py:39
  183.5 152.1 %while.22 = (s32[]{:T(128)}, f32[8,128,128]{2,0,1:T(8,128)S(1)}, s32[]{:T(128)}, s32[768]{0:T(1024)}, s32[]{:T(128)}, /*index=5*/bf16[768,128,128]{2,1,0:T(8,128...) while((s32[]{:T(128)}, f32[8,128,128]{2,0,1:T(8,128)S(1)}, ...), condition=%wide.region_3.4_spmd.clone, body=%wide.region_2.3_spmd.clone.sunk | while | flops 184682176 | bytes 9442623 | solution.py:66
  184.5 6.5 gather_fusion
  197.1 6.5 gather_fusion
  209.8 6.5 gather_fusion
  222.4 6.5 gather_fusion
  235.1 6.5 gather_fusion
  247.7 6.5 gather_fusion
  260.4 6.5 gather_fusion
  273.1 6.5 gather_fusion
  285.7 6.5 gather_fusion
  298.4 6.5 gather_fusion
  311.0 6.5 gather_fusion
  323.7 6.5 gather_fusion
  335.9 11.2 broadcast_in_dim.15
  347.2 123.3 %while.23 = (s32[]{:T(128)}, f32[512,128,128]{2,1,0:T(8,128)}, s32[]{:T(128)}, s32[768]{0:T(1024)}, bf16[768,128,128]{2,1,0:T(8,128)(2,1)}, /*index=5*/s32[768]{...) while((s32[]{:T(128)}, f32[512,128,128]{2,1,0:T(8,128)}, ...), condition=%wide.region_6.7_spmd.clone, body=%wide.region_4.6_spmd.clone.sunk | while | flops 135267616 | bytes 12588347 | solution.py:82
  470.5 70.5 %gather_fusion.3 = f32[16384,128]{1,0:T(8,128)} fusion(f32[65536,128]{1,0:T(8,128)} %bitcast.39, s32[16384]{0:T(1024)} %broadcast_clamp_fusion), kind=kCustom, calls=%fused_computation.3 | custom fusion | bytes 16842752 | tf_op jit(solution)/shard_map/gather | solution.py:88
  541.0 7.9 broadcast_multiply_fusion
  550.9 616.8 %reduce-scatter.5.cloned.1.call-done = f32[256,128]{1,0:T(8,128)} async-done(((f32[16384,128]{1,0:T(8,128)}), f32[256,128]{1,0:T(8,128)}) %reduce-scatter.5.cloned.1.call-update) | async-done | bytes 131088 | tf_op jit(solution)/shard_map/reduce_scatter | solution.py:89
  1170.2 7.1 all_gather.7
  1179.1 556.5 %all-reduce.2.cloned.1.call-done = f32[64,256]{1,0:T(8,128)} async-done(((f32[64,256]{1,0:T(8,128)}), f32[64,256]{1,0:T(8,128)}) %all-reduce.2.cloned.1.call-update) | async-done | bytes 65552 | tf_op jit(solution)/shard_map/psum | solution.py:100
  (197 shorter events, 210.6 us)
Async XLA Ops:
  7.2 13.8 copy-start
  7.2 13.8 copy-start.6
  7.2 15.2 copy-start.8
  7.2 44.1 %copy-start.9 = (s32[1024]{0:T(1024)S(1)}, s32[1024]{0:T(1024)}, u32[]{:S(2)}) copy-start(s32[1024]{0:T(1024)} %param.22) | copy-start | bytes 12292
  7.2 40.6 %reduce-scatter.3.cloned.1.call-start = ((), (), s32[]{:S(2)}) async-start(), calls=%async_computation.2 | async-start | bytes 1572864 | tf_op jit(solution)/shard_map/reduce_scatter | solution.py:31
  22.3 103.9 %all-gather.3.cloned.1.call-start = ((), (), s32[]{:S(2)}) async-start(), calls=%async_computation.5 | async-start | bytes 4259840 | tf_op jit(solution)/shard_map/all_gather | solution.py:38
  50.4 1117.3 %reduce-scatter.5.cloned.1.call-start = ((), (), s32[]{:S(2)}) async-start(), calls=%async_computation.3 | async-start | bytes 8519680 | tf_op jit(solution)/shard_map/reduce_scatter | solution.py:89
  52.8 129.9 %copy-start.3 = (f32[1024,128]{1,0:T(8,128)S(1)}, f32[1024,128]{1,0:T(8,128)}, u32[]{:S(2)}) copy-start(f32[1024,128]{1,0:T(8,128)} %reduce-scatter.3.cloned.1.call-done) | copy-start | bytes 1572868
  183.5 152.2 %copy-start.5 = (bf16[1024,128]{1,0:T(8,128)(2,1)S(1)}, bf16[1024,128]{1,0:T(8,128)(2,1)}, u32[]{:S(2)}) copy-start(bf16[1024,128]{1,0:T(8,128)(2,1)} %param.23) | copy-start | bytes 786436
  335.5 11.6 copy-start.1
  470.5 70.5 %copy-start.4 = (f32[8,2,8,128]{3,1,2,0:T(2,128)S(1)}, f32[8,2,8,128]{3,1,2,0:T(2,128)}, u32[]{:S(2)}) copy-start(f32[8,2,8,128]{3,1,2,0:T(2,128)} %copy.22) | copy-start | bytes 196612
  548.8 1.2 copy-start.2
  548.8 629.3 %copy-start.7 = (bf16[64,256]{1,0:T(8,128)(2,1)S(1)}, bf16[64,256]{1,0:T(8,128)(2,1)}, u32[]{:S(2)}) copy-start(bf16[64,256]{1,0:T(8,128)(2,1)} %param.15) | copy-start | bytes 98308
  548.9 1186.8 %all-reduce.2.cloned.1.call-start = ((), (), s32[]{:S(2)}) async-start(), calls=%async_computation.4 | async-start | bytes 131072 | tf_op jit(solution)/shard_map/psum | solution.py:100
Sparse Core Ops, SparseCore 0:
  22.5 25.3 reduce-scatter.2
  51.9 74.2 all-gather.2
  549.0 618.6 reduce-scatter.4
  1178.3 557.3 all-reduce.1
where the time goes:
time: 1750 us; the launch traced here: 1740 us
  waiting for transfers between devices  1270 us (73%)
  local copies, waits for them, and re-layouts  253 us (14%)
  other arithmetic  124 us (7%)
  matrix products  71.2 us (4%)
    reduce_scatter x1, waiting for transfers between devices, shards(): lax.psum_scatter(remote_terms.reshape(-1, width), 'dom', scatter_dimensio...  617 us
    psum x1, waiting for transfers between devices, shards(): grad_weight = lax.psum(local_weight, 'dom')  557 us
    gather x12, local copies, waits for them, and re-layouts, forward_step(): source_blocks[src_now]  78.2 us
    scatter-add x12, other arithmetic, backward_step(): return buffer.at[src_now].add(contrib * live_mask[:, None, None])  75.5 us
    all_gather x1, waiting for transfers between devices, shards(): arrived = lax.all_gather(picked, 'dom', axis=0, tiled=True)  73.5 us
    gather x1, local copies, waits for them, and re-layouts, shards(): flat_grads[global_rows].reshape(part_count, -1, width)  70.5 us
    scatter x1, local copies, waits for them, and re-layouts, shards(): source = stale_cache.at[global_rows].set(arrived)  56.4 us
  transfers between devices with their start and end apart: 4, of which 4 were waited for; matrix products, arithmetic and copies ran while one was open for 0% of the time, Pallas kernels for 0%

commit v1 on v0

v1 whole, which is shorter than its diff:
```python
import jax
import jax.numpy as jnp
from jax import lax
from jax.experimental import pallas as pl
from jax.experimental.pallas import tpu as pltpu
from jax.sharding import PartitionSpec as P

MESH = pl.DeviceIdType.MESH
BF16 = jnp.bfloat16
F32 = jnp.float32
I32 = jnp.int32

ROWS = 1024
REF = 256
TILE = 128
NT = 768
PARTS = 64
BLOCKS = PARTS * ROWS // TILE
PER = ROWS // TILE
RING = 4
CLASS = PARTS // 2
MIB = 1024 * 1024


def dot(lhs, rhs):
    return jnp.dot(lhs, rhs, preferred_element_type=F32)


class Place:
    def __init__(self):
        self.dom = lax.axis_index("dom")
        self.feat = lax.axis_index("feat")
        self.core = self.dom % 2
        self.z = (self.dom // 2) % 2
        self.y = (self.dom // 4) % RING
        self.x = self.dom // 16
        self.a = self.x * (1 - self.core) + self.y * self.core
        self.b = self.y * (1 - self.core) + self.x * self.core
        self.sibling = self.dom + 1 - 2 * self.core
        self.z_pair = self.dom + 2 - 4 * self.z
        self.a_next = self.at(self.a + 1, self.b)
        self.a_prev = self.at(self.a + 3, self.b)
        self.b_next = self.at(self.a, self.b + 1)
        self.b_prev = self.at(self.a, self.b + 3)

    def at(self, a, b):
        a, b = a % RING, b % RING
        x = a * (1 - self.core) + b * self.core
        y = b * (1 - self.core) + a * self.core
        return ((x * RING + y) * 2 + self.z) * 2 + self.core

    def xy(self, x, y):
        return (((x % RING) * RING + y % RING) * 2 + self.z) * 2 + self.core

    def slot(self, a, b, z):
        return self.core * CLASS + (b % RING) * 8 + (a % RING) * 2 + z

    def greet(self):
        barrier = pltpu.get_barrier_semaphore()
        near = (self.sibling, self.z_pair, self.a_next, self.a_prev, self.b_next, self.b_prev)
        for device in near:
            pl.semaphore_signal(barrier, inc=1, device_id=(device, self.feat), device_id_type=MESH)
        pl.semaphore_signal(
            barrier, inc=1, device_id=(self.dom, 1 - self.feat), device_id_type=MESH
        )
        return lambda: pl.semaphore_wait(barrier, len(near) + 1)


def slot_part(slot):
    core, b, a, z = slot // CLASS, (slot // 8) % RING, (slot // 2) % RING, slot % 2
    x = a * (1 - core) + b * core
    y = b * (1 - core) + a * core
    return ((x * RING + y) * 2 + z) * 2 + core


def part_slot(part):
    core, z, y, x = part % 2, (part // 2) % 2, (part // 4) % RING, part // 16
    a = x * (1 - core) + y * core
    b = y * (1 - core) + x * core
    return core * CLASS + b * 8 + a * 2 + z


def rows_by_refresh(row):
    column = jnp.transpose(jnp.broadcast_to(row, (TILE, REF)))
    lanes = lax.broadcasted_iota(I32, (REF, TILE), 1)
    parts = [(column == lanes + k * TILE).astype(F32).astype(BF16) for k in range(PER)]
    return jnp.concatenate(parts, axis=1)


def refresh_by_rows(row):
    rows = lax.broadcasted_iota(I32, (ROWS, REF), 0)
    return (rows == row).astype(F32).astype(BF16)


def gather_kernel(
    feat_ref,
    w_ref,
    refresh_ref,
    arr_out,
    fx_out,
    wcol_out,
    arr,
    pick,
    pick_in,
    wide,
    wide_in,
    wcol,
    send_sem,
    recv_sem,
    pair_send,
    pair_recv,
    out_sem,
):
    me = Place()
    ready = me.greet()
    f = me.feat
    spread_to = lax.broadcasted_iota(I32, (64, TILE), 1)
    spread_from = lax.broadcasted_iota(I32, (64, TILE), 0)
    spread = (spread_to == spread_from + f * 64).astype(F32).astype(BF16)
    wide[...] = dot(feat_ref[...], spread).astype(BF16)
    chosen = rows_by_refresh(refresh_ref[pl.ds(me.dom, 1), :])
    pick[...] = dot(chosen, wide[...]).astype(BF16)
    ready()

    def to_pair(k, src, dst):
        return pltpu.make_async_remote_copy(
            src_ref=src,
            dst_ref=dst,
            send_sem=pair_send.at[k],
            recv_sem=pair_recv.at[k],
            device_id=(me.dom, 1 - f),
            device_id_type=MESH,
        )

    own_columns = pl.ds(pl.multiple_of(f * TILE, TILE), TILE)
    pair_columns = pl.ds(pl.multiple_of((1 - f) * TILE, TILE), TILE)
    own_rows = pl.ds(pl.multiple_of(f * 64, 64), 64)
    pick_copy = to_pair(0, pick, pick_in)
    pick_copy.start()
    w_copy = to_pair(1, w_ref.at[:, pair_columns], wcol.at[own_rows, :])
    w_copy.start()
    wide_copy = to_pair(2, wide, wide_in)
    wide_copy.start()
    wcol_out[own_rows, :] = w_ref[:, own_columns]

    sends = []

    def send(slot, target):
        copy = pltpu.make_async_remote_copy(
            src_ref=arr.at[slot],
            dst_ref=arr.at[slot],
            send_sem=send_sem.at[len(sends)],
            recv_sem=recv_sem.at[slot],
            device_id=(target, f),
            device_id_type=MESH,
        )
        copy.start()
        sends.append(copy)

    def arrive(slot):
        pltpu.make_async_remote_copy(
            src_ref=arr.at[slot],
            dst_ref=arr.at[slot],
            send_sem=send_sem.at[0],
            recv_sem=recv_sem.at[slot],
            device_id=(me.sibling, f),
            device_id_type=MESH,
        ).wait_recv()

    a, b, z, o = me.a, me.b, me.z, 1 - me.z
    mine = me.slot(a, b, z)
    pick_copy.wait_recv()
    arr[pl.ds(mine, 1)] = (pick[...] + pick_in[...])[None]

    def spread_b(slot):
        send(slot, me.b_next)
        send(slot, me.b_prev)
        send(slot, me.sibling)

    send(mine, me.z_pair)
    send(mine, me.a_next)
    send(mine, me.a_prev)
    spread_b(mine)

    slot = me.slot(a, b, o)
    arrive(slot)
    send(slot, me.a_next)
    send(slot, me.a_prev)
    spread_b(slot)

    slot = me.slot(a + 3, b, z)
    arrive(slot)
    send(slot, me.a_next)
    spread_b(slot)
    slot = me.slot(a + 1, b, z)
    arrive(slot)
    spread_b(slot)

    def ring_b(aa, zz):
        slot = me.slot(aa, b + 3, zz)
        arrive(slot)
        if zz is z:
            send(slot, me.b_next)
        send(slot, me.sibling)
        slot = me.slot(aa, b + 1, zz)
        arrive(slot)
        if zz is not z:
            send(slot, me.b_prev)
        send(slot, me.sibling)

    ring_b(a, z)
    slot = me.slot(a + 3, b, o)
    arrive(slot)
    spread_b(slot)
    slot = me.slot(a + 1, b, o)
    arrive(slot)
    send(slot, me.a_prev)
    spread_b(slot)
    ring_b(a, o)
    slot = me.slot(a + 2, b, z)
    arrive(slot)
    spread_b(slot)
    slot = me.slot(a + 2, b, o)
    arrive(slot)
    spread_b(slot)
    ring_b(a + 3, z)
    ring_b(a + 1, z)
    ring_b(a + 3, o)
    ring_b(a + 1, o)
    ring_b(a + 2, z)
    ring_b(a + 2, o)
    for aa, zz in (
        (a, z),
        (a, o),
        (a + 3, z),
        (a + 1, z),
        (a + 3, o),
        (a + 1, o),
        (a + 2, z),
        (a + 2, o),
    ):
        slot = me.slot(aa, b + 2, zz)
        arrive(slot)
        send(slot, me.sibling)

    def keep(k, first):
        part = pl.ds(first, CLASS)
        return pltpu.make_async_copy(arr.at[part], arr_out.at[part], out_sem.at[k])

    keep_own = keep(0, me.core * CLASS)
    keep_own.start()
    wide_copy.wait_recv()
    fx_out[...] = wide[...] + wide_in[...]
    w_copy.wait_recv()
    wcol_out[pl.ds(pl.multiple_of((1 - f) * 64, 64), 64), :] = wcol[
        pl.ds(pl.multiple_of((1 - f) * 64, 64), 64), :
    ]
    other = (1 - me.core) * CLASS
    for k in range(CLASS):
        arrive(other + k)
    keep_other = keep(1, other)
    keep_other.start()
    for copy in sends:
        copy.wait_send()
    pick_copy.wait_send()
    w_copy.wait_send()
    wide_copy.wait_send()
    keep_own.wait()
    keep_other.wait()


CHUNK = 12
AHEAD = 10
UNROLL = 8


def forward_kernel(
    src_ref,
    dst_ref,
    count_ref,
    refresh_ref,
    fx_ref,
    wcol_ref,
    mask_ref,
    gh_ref,
    arr_hbm,
    stale_hbm,
    tiles_hbm,
    hidden_ref,
    delta_ref,
    source,
    tiles,
    arr,
    acc,
    stale_sem,
    arr_sem,
    tile_sem,
):
    me = lax.axis_index("dom")
    live = count_ref[0]

    def stale_copy(slot):
        rows = pl.ds(pl.multiple_of(slot_part(slot) * ROWS, ROWS), ROWS)
        return pltpu.make_async_copy(stale_hbm.at[rows], source.at[rows], stale_sem.at[slot])

    def arr_copy(slot):
        return pltpu.make_async_copy(arr_hbm.at[slot], arr.at[slot], arr_sem.at[slot])

    def tile_copy(chunk):
        part = pl.ds(chunk * CHUNK, CHUNK)
        return pltpu.make_async_copy(tiles_hbm.at[part], tiles.at[part], tile_sem.at[chunk])

    def first(slot, carry):
        stale_copy(slot).start()
        arr_copy(slot).start()
        return carry

    lax.fori_loop(0, AHEAD, first, 0)
    acc[...] = jnp.zeros_like(acc)
    wcol = wcol_ref[...]
    ones = jnp.ones((REF, TILE), BF16)

    def merge(slot, carry):
        @pl.when(slot + AHEAD < PARTS)
        def _():
            stale_copy(slot + AHEAD).start()
            arr_copy(slot + AHEAD).start()

        @pl.when(slot * CHUNK < live)
        def _():
            tile_copy(slot).start()

        part = slot_part(slot)
        arr_copy(slot).wait()
        fresh = dot(arr[pl.ds(slot, 1)][0], wcol).astype(BF16)
        chosen = refresh_by_rows(refresh_ref[pl.ds(part, 1), :])
        placed = dot(chosen, jnp.concatenate([fresh, ones], axis=1))
        stale_copy(slot).wait()
        rows = pl.ds(pl.multiple_of(part * ROWS, ROWS), ROWS)
        old = source[rows, :].astype(F32)
        source[rows, :] = jnp.where(placed[:, TILE:] > 0, placed[:, :TILE], old).astype(BF16)
        return carry

    lax.fori_loop(0, PARTS, merge, 0)
    own = pl.ds(pl.multiple_of(me * ROWS, ROWS), ROWS)
    source[own, :] = dot(fx_ref[...], wcol).astype(BF16)

    def wait_chunk(chunk, carry):
        tile_copy(chunk).wait()
        return carry

    lax.fori_loop(0, (live + CHUNK - 1) // CHUNK, wait_chunk, 0)

    def step(index, carry):
        for k in range(UNROLL):
            t = index * UNROLL + k
            rows = pl.ds(pl.multiple_of(src_ref[t] * TILE, TILE), TILE)
            product = dot(tiles[t], source[rows, :])
            d = jnp.where(t < live, dst_ref[t], PER)
            acc[pl.ds(d, 1)] = acc[pl.ds(d, 1)] + product[None]
        return carry

    lax.fori_loop(0, (live + UNROLL - 1) // UNROLL, step, 0)

    for d in range(PER):
        pre = acc[d]
        rows = pl.ds(d * TILE, TILE)
        hidden_ref[rows, :] = jnp.maximum(pre, 0.0).astype(BF16)
        passed = jnp.where(pre > 0, gh_ref[rows, :].astype(F32), 0.0)
        kept = mask_ref[pl.ds(d, 1), :].astype(F32)
        delta_ref[d] = (jnp.transpose(passed) * kept).astype(BF16)


B_CHUNK = 32
B_RING = 4


def backward_kernel(
    src_ref,
    dst_ref,
    count_ref,
    refresh_ref,
    fx_ref,
    delta_ref,
    arr_hbm,
    tiles_hbm,
    picked_hbm,
    own_ref,
    gw_ref,
    acc,
    tiles,
    arr,
    picked,
    gw_total,
    tile_sem,
    arr_sem,
    out_sem,
):
    me = lax.axis_index("dom")
    live = count_ref[0]
    chunks = (live + B_CHUNK - 1) // B_CHUNK

    def tile_copy(chunk):
        part = pl.ds(chunk * B_CHUNK, B_CHUNK)
        place = chunk % B_RING
        return pltpu.make_async_copy(tiles_hbm.at[part], tiles.at[place], tile_sem.at[place])

    for k in range(B_RING - 1):

        @pl.when(k < chunks)
        def _():
            tile_copy(k).start()

    arr_copy = pltpu.make_async_copy(arr_hbm, arr, arr_sem)
    arr_copy.start()

    def clear(block, carry):
        acc[pl.ds(block, 1)] = jnp.zeros((1, TILE, TILE), F32)
        return carry

    lax.fori_loop(0, BLOCKS + 1, clear, 0)

    def take_chunk(chunk, carry):
        @pl.when(chunk + B_RING - 1 < chunks)
        def _():
            tile_copy(chunk + B_RING - 1).start()

        tile_copy(chunk).wait()
        place = chunk % B_RING

        def step(index, carry):
            for k in range(UNROLL):
                local = index * UNROLL + k
                t = chunk * B_CHUNK + local
                product = dot(delta_ref[dst_ref[t]], tiles[place, local])
                s = jnp.where(t < live, src_ref[t], BLOCKS)
                acc[pl.ds(s, 1)] = acc[pl.ds(s, 1)] + product[None]
            return carry

        return lax.fori_loop(0, B_CHUNK // UNROLL, step, carry)

    lax.fori_loop(0, chunks, take_chunk, 0)
    arr_copy.wait()
    gw_total[...] = jnp.zeros_like(gw_total)

    def out_copy(slot):
        return pltpu.make_async_copy(picked.at[slot], picked_hbm.at[slot], out_sem.at[slot])

    def pick(slot, carry):
        part = slot_part(slot)
        chosen = refresh_by_rows(refresh_ref[pl.ds(part, 1), :])
        blocks = [acc[part * PER + k].astype(BF16) for k in range(PER)]
        grads = dot(jnp.concatenate(blocks, axis=1), chosen)
        grads = jnp.where(part == me, 0.0, grads).astype(BF16)
        picked[pl.ds(slot, 1)] = grads[None]
        out_copy(slot).start()
        gw_total[...] += dot(grads, arr[pl.ds(slot, 1)][0])
        return carry

    lax.fori_loop(0, PARTS, pick, 0)
    for k in range(PER):
        own_ref[:, pl.ds(k * TILE, TILE)] = acc[me * PER + k]
    gw = gw_total[...] + dot(own_ref[...].astype(BF16), fx_ref[...])
    gw_ref[...] = jnp.transpose(gw)

    def wait_out(slot, carry):
        out_copy(slot).wait()
        return carry

    lax.fori_loop(0, PARTS, wait_out, 0)


def scatter_kernel(
    refresh_ref,
    w_ref,
    own_ref,
    gw_ref,
    picked_hbm,
    gf_out,
    gw_out,
    work,
    sib,
    from_b1,
    from_b2,
    from_a1,
    from_a2,
    from_z,
    sums,
    sums_in,
    gw_in,
    grad,
    grad_in,
    load_sem,
    send_sem,
    recv_sem,
):
    me = Place()
    ready = me.greet()
    f, a, b, z = me.feat, me.a, me.b, me.z
    loads = []
    for k, chunk in enumerate((b + 2, b + 1, b + 3, b)):
        first = (chunk % RING) * 8
        copy = pltpu.make_async_copy(
            picked_hbm.at[pl.ds(me.core * CLASS + first, 8)],
            work.at[pl.ds(first, 8)],
            load_sem.at[k],
        )
        copy.start()
        loads.append(copy)
    sums[0] = gw_ref[...]
    ready()
    sends = []

    def send(src, dst, target, feat=None):
        k = len(sends)
        copy = pltpu.make_async_remote_copy(
            src_ref=src,
            dst_ref=dst,
            send_sem=send_sem.at[k],
            recv_sem=recv_sem.at[k],
            device_id=(target, f if feat is None else feat),
            device_id_type=MESH,
        )
        copy.start()
        sends.append(copy)
        return copy

    y_one = me.xy(me.x, me.y + 1 + 2 * (me.y % 2))
    y_two = me.xy(me.x, me.y + 3 - 2 * (me.y % 2))
    x_one = me.xy(me.x + 1 + 2 * (me.x % 2), me.y)
    x_two = me.xy(me.x + 3 - 2 * (me.x % 2), me.y)
    partners = (me.sibling, y_one, y_two, x_one, x_two, me.z_pair)

    def sum_send(k):
        return send(sums.at[k], sums_in.at[k], partners[k])

    def sum_take(k, copy):
        copy.wait_recv()
        sums[k + 1] = sums[k] + sums_in[k]

    def add(ref, first, size, *others):
        part = pl.ds(first, size)
        total = ref[part].astype(F32)
        for other in others:
            total = total + other.astype(F32)
        ref[part] = total.astype(BF16)

    gw_copy = sum_send(0)
    to_sib = []
    for chunk in (a + 2, a + 1, a + 3, a):
        first = (chunk % RING) * 8
        src = picked_hbm.at[pl.ds((1 - me.core) * CLASS + first, 8)]
        to_sib.append(send(src, sib.at[pl.ds(first, 8)], me.sibling))

    def fold(k, chunk):
        first = (chunk % RING) * 8
        loads[k].wait()
        to_sib[k].wait_recv()
        add(work, first, 8, sib[pl.ds(first, 8)])
        return first

    across = fold(0, b + 2)
    b1_up = send(work.at[pl.ds(across, 4)], from_b1.at[pl.ds(0, 4)], me.b_next)
    b1_down = send(work.at[pl.ds(across + 4, 4)], from_b1.at[pl.ds(4, 4)], me.b_prev)
    up = fold(1, b + 1)
    b2_up_late = send(work.at[pl.ds(up + 4, 4)], from_b2.at[0, pl.ds(4, 4)], me.b_next)
    down = fold(2, b + 3)
    b2_down_early = send(work.at[pl.ds(down, 4)], from_b2.at[1, pl.ds(0, 4)], me.b_prev)
    sum_take(0, gw_copy)
    gw_copy = sum_send(1)
    here = fold(3, b)
    b1_up.wait_recv()
    add(work, up, 4, from_b1[pl.ds(0, 4)])
    b2_up_early = send(work.at[pl.ds(up, 4)], from_b2.at[0, pl.ds(0, 4)], me.b_next)
    b1_down.wait_recv()
    add(work, down + 4, 4, from_b1[pl.ds(4, 4)])
    b2_down_late = send(work.at[pl.ds(down + 4, 4)], from_b2.at[1, pl.ds(4, 4)], me.b_prev)
    sum_take(1, gw_copy)
    gw_copy = sum_send(2)
    sum_take(2, gw_copy)
    gw_copy = sum_send(3)
    b2_up_late.wait_recv()
    b2_down_early.wait_recv()
    b2_up_early.wait_recv()
    b2_down_late.wait_recv()
    add(work, here, 8, from_b2[0], from_b2[1])

    across = here + ((a + 2) % RING) * 2
    up = here + ((a + 1) % RING) * 2
    down = here + ((a + 3) % RING) * 2
    mine = here + a * 2
    a1_up = send(work.at[pl.ds(across, 1)], from_a1.at[pl.ds(0, 1)], me.a_next)
    a1_down = send(work.at[pl.ds(across + 1, 1)], from_a1.at[pl.ds(1, 1)], me.a_prev)
    a2_up_late = send(work.at[pl.ds(up + 1, 1)], from_a2.at[0, pl.ds(1, 1)], me.a_next)
    a2_down_early = send(work.at[pl.ds(down, 1)], from_a2.at[1, pl.ds(0, 1)], me.a_prev)
    sum_take(3, gw_copy)
    gw_copy = sum_send(4)
    a1_up.wait_recv()
    add(work, up, 1, from_a1[pl.ds(0, 1)])
    a2_up_early = send(work.at[pl.ds(up, 1)], from_a2.at[0, pl.ds(0, 1)], me.a_next)
    a1_down.wait_recv()
    add(work, down + 1, 1, from_a1[pl.ds(1, 1)])
    a2_down_late = send(work.at[pl.ds(down + 1, 1)], from_a2.at[1, pl.ds(1, 1)], me.a_prev)
    chosen = rows_by_refresh(refresh_ref[pl.ds(me.dom, 1), :])
    sum_take(4, gw_copy)
    gw_copy = sum_send(5)
    a2_up_late.wait_recv()
    a2_down_early.wait_recv()
    a2_up_early.wait_recv()
    a2_down_late.wait_recv()
    add(work, mine, 2, from_a2[0], from_a2[1])
    z_copy = send(work.at[pl.ds(mine + 1 - z, 1)], from_z, me.z_pair)
    sum_take(5, gw_copy)
    other_rows = pl.ds(pl.multiple_of((1 - f) * 64, 64), 64)
    own_rows = pl.ds(pl.multiple_of(f * 64, 64), 64)
    swap = send(sums.at[6, other_rows, :], gw_in, me.dom, 1 - f)
    z_copy.wait_recv()
    carried = work[pl.ds(mine + z, 1)][0].astype(F32) + from_z[0].astype(F32)
    grad[...] = (own_ref[...] + dot(carried.astype(BF16), chosen)).astype(BF16)
    grad_copy = send(grad, grad_in, me.dom, 1 - f)
    own_columns = pl.ds(pl.multiple_of(f * TILE, TILE), TILE)
    other_columns = pl.ds(pl.multiple_of((1 - f) * TILE, TILE), TILE)
    half = dot(w_ref[:, own_columns], grad[...])
    swap.wait_recv()
    gw_out[:, own_columns] = sums[6, own_rows, :]
    gw_out[:, other_columns] = gw_in[...]
    grad_copy.wait_recv()
    half = half + dot(w_ref[:, other_columns], grad_in[...])
    gf_out[...] = jnp.transpose(half).astype(BF16)
    for copy in sends:
        copy.wait_send()


VMEM = pl.BlockSpec(memory_space=pltpu.VMEM)
SMEM = pl.BlockSpec(memory_space=pltpu.SMEM)
ANY = pl.BlockSpec(memory_space=pl.ANY)
DMA = pltpu.SemaphoreType.DMA


def shape(dims, kind):
    return jax.ShapeDtypeStruct(dims, kind)


def shards(
    features,
    weight,
    stale_cache,
    adj_tiles,
    tile_src,
    tile_dst,
    tile_count,
    refresh,
    train_mask,
    grad_hidden,
):
    arr, fx, wcol = pl.pallas_call(
        gather_kernel,
        out_shape=(
            shape((PARTS, REF, TILE), BF16),
            shape((ROWS, TILE), BF16),
            shape((TILE, TILE), BF16),
        ),
        in_specs=[VMEM, VMEM, VMEM],
        out_specs=(ANY, VMEM, VMEM),
        scratch_shapes=[
            pltpu.VMEM((PARTS, REF, TILE), BF16),
            pltpu.VMEM((REF, TILE), BF16),
            pltpu.VMEM((REF, TILE), BF16),
            pltpu.VMEM((ROWS, TILE), BF16),
            pltpu.VMEM((ROWS, TILE), BF16),
            pltpu.VMEM((TILE, TILE), BF16),
            DMA((63,)),
            DMA((PARTS,)),
            DMA((3,)),
            DMA((3,)),
            DMA((2,)),
        ],
        compiler_params=pltpu.CompilerParams(
            collective_id=0, has_side_effects=True, vmem_limit_bytes=32 * MIB
        ),
        name="gather_refreshed",
    )(features, weight, refresh)
    hidden, delta = pl.pallas_call(
        forward_kernel,
        out_shape=(shape((ROWS, TILE), BF16), shape((PER, TILE, TILE), BF16)),
        in_specs=[SMEM, SMEM, SMEM, VMEM, VMEM, VMEM, VMEM, VMEM, ANY, ANY, ANY],
        out_specs=(VMEM, VMEM),
        scratch_shapes=[
            pltpu.VMEM((PARTS * ROWS, TILE), BF16),
            pltpu.VMEM((NT, TILE, TILE), BF16),
            pltpu.VMEM((PARTS, REF, TILE), BF16),
            pltpu.VMEM((PER + 1, TILE, TILE), F32),
            DMA((PARTS,)),
            DMA((PARTS,)),
            DMA((NT // CHUNK,)),
        ],
        compiler_params=pltpu.CompilerParams(vmem_limit_bytes=60 * MIB),
        name="forward_tiles",
    )(
        tile_src,
        tile_dst,
        tile_count,
        refresh,
        fx,
        wcol,
        train_mask.reshape(PER, TILE),
        grad_hidden,
        arr,
        stale_cache,
        adj_tiles,
    )
    picked, own, gw = pl.pallas_call(
        backward_kernel,
        out_shape=(
            shape((PARTS, TILE, REF), BF16),
            shape((TILE, ROWS), F32),
            shape((TILE, TILE), F32),
        ),
        in_specs=[SMEM, SMEM, SMEM, VMEM, VMEM, VMEM, ANY, ANY],
        out_specs=(ANY, VMEM, VMEM),
        scratch_shapes=[
            pltpu.VMEM((BLOCKS + 1, TILE, TILE), F32),
            pltpu.VMEM((B_RING, B_CHUNK, TILE, TILE), BF16),
            pltpu.VMEM((PARTS, REF, TILE), BF16),
            pltpu.VMEM((PARTS, TILE, REF), BF16),
            pltpu.VMEM((TILE, TILE), F32),
            DMA((B_RING,)),
            DMA,
            DMA((PARTS,)),
        ],
        compiler_params=pltpu.CompilerParams(vmem_limit_bytes=60 * MIB),
        name="backward_tiles",
    )(tile_src, tile_dst, tile_count, refresh, fx, delta, arr, adj_tiles)
    grad_features, grad_weight = pl.pallas_call(
        scatter_kernel,
        out_shape=(shape((ROWS, 64), BF16), shape((64, 2 * TILE), F32)),
        in_specs=[VMEM, VMEM, VMEM, VMEM, ANY],
        out_specs=(VMEM, VMEM),
        scratch_shapes=[
            pltpu.VMEM((CLASS, TILE, REF), BF16),
            pltpu.VMEM((CLASS, TILE, REF), BF16),
            pltpu.VMEM((8, TILE, REF), BF16),
            pltpu.VMEM((2, 8, TILE, REF), BF16),
            pltpu.VMEM((2, TILE, REF), BF16),
            pltpu.VMEM((2, 2, TILE, REF), BF16),
            pltpu.VMEM((1, TILE, REF), BF16),
            pltpu.VMEM((7, TILE, TILE), F32),
            pltpu.VMEM((6, TILE, TILE), F32),
            pltpu.VMEM((64, TILE), F32),
            pltpu.VMEM((TILE, ROWS), BF16),
            pltpu.VMEM((TILE, ROWS), BF16),
            DMA((4,)),
            DMA((32,)),
            DMA((32,)),
        ],
        compiler_params=pltpu.CompilerParams(
            collective_id=1, has_side_effects=True, vmem_limit_bytes=32 * MIB
        ),
        name="scatter_gradients",
    )(refresh, weight, own, gw, picked)
    return hidden, grad_features, grad_weight


def solution(mesh):
    placed = (
        P("dom", "feat"),
        P("feat", None),
        P(None, "feat"),
        P("dom", None, None),
        P("dom"),
        P("dom"),
        P("dom"),
        P(),
        P("dom"),
        P("dom", "feat"),
    )
    return jax.shard_map(
        shards,
        mesh=mesh,
        in_specs=placed,
        out_specs=(P("dom", "feat"), P("dom", "feat"), P("feat", None)),
        check_vma=False,
    )
```

time: 1750 us -> 201 us (0.11)
  waiting for transfers between devices: 1270 us -> 0 us
  local copies, waits for them, and re-layouts: 253 us -> 11.4 us
  Pallas kernels: 0 us -> 187 us
  other arithmetic: 124 us -> 0 us
  matrix products: 71.2 us -> 0 us
    reduce_scatter x2 -> x0, waiting for transfers between devices: 642 us -> none  [the longest x1 617 us: shards(): lax.psum_scatter(remote_terms.reshape(-1, width), 'dom', scatter_dimensio...]
    psum x1 -> x0, waiting for transfers between devices: 557 us -> none  [shards(): grad_weight = lax.psum(local_weight, 'dom')]
    pallas_call x0 -> x4, Pallas kernels: none -> 187 us  [the longest x1 69.8 us: shards(): pl.pallas_call(scatter_kernel, out_shape=(shape((ROWS, 64), BF16), shape(...]
    gather x26 -> x0, local copies, waits for them, and re-layouts: 159 us -> none  [the longest x12 78.2 us: forward_step(): source_blocks[src_now]]
    scatter-add x13 -> x0, other arithmetic: 78 us -> none  [the longest x12 75.5 us: backward_step(): return buffer.at[src_now].add(contrib * live_mask[:, None, None])]
    all_gather x1 -> x0, waiting for transfers between devices: 73.5 us -> none  [shards(): arrived = lax.all_gather(picked, 'dom', axis=0, tiled=True)]
    dot_general x39 -> x0, matrix products: 71.2 us -> none  [the longest x12 27 us: forward_step(): jnp.einsum('tb,tic->bic', onehot, product, precision=highest)]
    scatter x1 -> x0, local copies, waits for them, and re-layouts: 56.4 us -> none  [shards(): source = stale_cache.at[global_rows].set(arrived)]
  transfers between devices with their start and end apart: 4 -> 0, of which waited for: 4 -> 0; matrix products, arithmetic and copies ran while one was open for 0% -> 0% of each run, Pallas kernels for 0% -> 0%
where the time goes in v1:
time: 201 us; the launch traced here: 200 us
  Pallas kernels  187 us (93%)
  local copies, waits for them, and re-layouts  11.4 us (6%)
    pallas_call x1, Pallas kernels, shards(): pl.pallas_call(scatter_kernel, out_shape=(shape((ROWS, 64), BF16), shape(...  69.8 us
    pallas_call x1, Pallas kernels, shards(): pl.pallas_call(forward_kernel, out_shape=(shape((ROWS, TILE), BF16), shap...  45.6 us
    pallas_call x1, Pallas kernels, shards(): pl.pallas_call(backward_kernel, out_shape=(shape((PARTS, TILE, REF), BF16...  38.1 us
    pallas_call x1, Pallas kernels, shards(): pl.pallas_call(gather_kernel, out_shape=(shape((PARTS, REF, TILE), BF16),...  33.6 us
    unnamed x23, local copies, waits for them, and re-layouts  11.4 us

profile of v1, /device:TPU:0, one launch (start us, length us, event | category | flops | bytes accessed | tf_op | source)
XLA Modules:
  0.0 200.0 jit_solution(16149081805234928717)
XLA Ops:
  1.3 1.1 copy.13.feat_ref
  2.4 0.0 copy-start.3
  2.4 0.8 copy-done.3
  3.2 0.0 copy-start.6
  3.2 0.8 copy-done.6
  4.0 33.6 %gather_refreshed.1 = (bf16[64,256,128]{2,1,0:T(8,128)(2,1)S(1)}, bf16[1024,128]{1,0:T(8,128)(2,1)S(1)}, bf16[128,128]{1,0:T(8,128)(2,1)S(1)}) custom-call(bf16[1024,64]{1,0:T(8,128)(2,1)S(1)} %copy.13.feat_ref, bf16[64,256]{1,0:T(8,128)(2,1)S(1)} %copy-done.6, s32[64,256]{1,0:T(8,128)S(1)} %copy-done.3), custom_call_target="tpu_custom_call" | custom-call | tf_op jit(solution)/shard_map/gather_refreshed/pallas_call | solution.py:656
  37.6 0.0 copy-start
  37.6 1.9 copy-done
  39.5 0.0 copy-start.2
  39.5 0.7 copy-done.2
  40.3 0.6 copy-done.9
  40.9 45.6 %forward_tiles.1 = (bf16[1024,128]{1,0:T(8,128)(2,1)}, bf16[8,128,128]{2,1,0:T(8,128)(2,1)}) custom-call(s32[768]{0:T(1024)} %src_ref.3, s32[768]{0:T(1024)} %dst_ref.3, s32[1]{0:T(128)S(6)} %copy.16.count_ref, s32[64,256]{1,0:T(8,128)} %refresh_ref.7, bf16[1024,128]{1,0:T(8,128)(2,1)} %copy-done.2, bf16[128,128]{1,0:T(8,128)(2,1)} %copy-done.9, ...), custom_call_target="tpu_custom_call" | custom-call | tf_op jit(solution)/shard_map/forward_tiles/pallas_call | solution.py:683
  86.5 0.0 copy-start.4
  86.5 0.0 copy-start.7
  86.5 38.1 %backward_tiles.1 = (bf16[64,128,256]{2,1,0:T(8,128)(2,1)}, f32[128,1024]{1,0:T(8,128)}, f32[128,128]{1,0:T(8,128)}) custom-call(s32[768]{0:T(1024)} %src_ref.3, s32[768]{0:T(1024)} %dst_ref.3, s32[1]{0:T(128)S(6)} %copy.16.count_ref, s32[64,256]{1,0:T(8,128)} %refresh_ref.7, bf16[1024,128]{1,0:T(8,128)(2,1)} %copy-done.2, ...), custom_call_target="tpu_custom_call" | custom-call | tf_op jit(solution)/shard_map/backward_tiles/pallas_call | solution.py:712
  124.7 0.0 copy-done.4
  124.7 0.0 copy-done.7
  124.7 0.0 copy-start.1
  124.7 2.2 %copy-done.1 = bf16[64,128,256]{2,1,0:T(8,128)(2,1)S(1)} copy-done((bf16[64,128,256]{2,1,0:T(8,128)(2,1)S(1)}, bf16[64,128,256]{2,1,0:T(8,128)(2,1)}, u32[]{:S(2)}) %copy-start.1) | copy-done | bytes 4194328
  126.9 1.0 copy-done.5
  127.9 0.8 copy-done.8
  128.8 69.8 %scatter_gradients.1 = (bf16[1024,64]{1,0:T(8,128)(2,1)S(1)}, f32[64,256]{1,0:T(8,128)S(1)}) custom-call(s32[64,256]{1,0:T(8,128)S(1)} %copy-done.4, bf16[64,256]{1,0:T(8,128)(2,1)S(1)} %copy-done.7, f32[128,1024]{1,0:T(8,128)S(1)} %copy-done.5, f32[128,128]{1,0:T(8,128)S(1)} %copy-done.8, bf16[64,128,256]{2,1,0:T(8,128)(2,1)S(1)} %copy-done.1), custom_call_target="tpu_custom_call" | custom-call | tf_op jit(solution)/shard_map/scatter_gradients/pallas_call | solution.py:734
  198.5 0.8 copy.14
  199.3 0.6 copy.17
  (3 shorter events, 0.0 us)
Async XLA Ops:
  2.4 0.8 copy-start.3
  3.2 0.8 copy-start.6
  37.6 1.9 copy-start
  39.5 0.7 copy-start.2
  40.3 0.6 copy-start.9
  86.5 38.2 %copy-start.4 = (s32[64,256]{1,0:T(8,128)S(1)}, s32[64,256]{1,0:T(8,128)}, u32[]{:S(2)}) copy-start(s32[64,256]{1,0:T(8,128)} %refresh_ref.7) | copy-start | bytes 196612
  86.5 38.1 %copy-start.7 = (bf16[64,256]{1,0:T(8,128)(2,1)S(1)}, bf16[64,256]{1,0:T(8,128)(2,1)}, u32[]{:S(2)}) copy-start(bf16[64,256]{1,0:T(8,128)(2,1)} %w_ref.3) | copy-start | bytes 98308
  124.7 2.2 %copy-start.1 = (bf16[64,128,256]{2,1,0:T(8,128)(2,1)S(1)}, bf16[64,128,256]{2,1,0:T(8,128)(2,1)}, u32[]{:S(2)}) copy-start(bf16[64,128,256]{2,1,0:T(8,128)(2,1)} %get-tuple-element.20.picked_hbm) | copy-start | bytes 12582916
  126.9 1.0 copy-start.5
  127.9 0.8 copy-start.8

commit v2 on v1

--- a/solution.py
+++ b/solution.py
@@ -92,34 +92,55 @@
     return (rows == row).astype(F32).astype(BF16)
 
 
+def fetch(sems, *pairs):
+    copies = [pltpu.make_async_copy(src, dst, sems.at[k]) for k, (src, dst) in enumerate(pairs)]
+    for copy in copies:
+        copy.start()
+    return copies
+
+
+def half_rows(index):
+    return pl.ds(pl.multiple_of(index * 64, 64), 64)
+
+
+def column_block(index):
+    return pl.ds(pl.multiple_of(index * TILE, TILE), TILE)
+
+
 def gather_kernel(
-    feat_ref,
-    w_ref,
-    refresh_ref,
+    feat_hbm,
+    w_hbm,
+    refresh_hbm,
     arr_out,
     fx_out,
     wcol_out,
     arr,
     pick,
-    pick_in,
-    wide,
-    wide_in,
+    fx,
+    weight,
     wcol,
+    refresh,
     send_sem,
     recv_sem,
     pair_send,
     pair_recv,
+    load_sem,
     out_sem,
 ):
     me = Place()
+    f = me.feat
+    own_rows, pair_rows = half_rows(f), half_rows(1 - f)
+    own_columns, pair_columns = column_block(f), column_block(1 - f)
+    loads = fetch(
+        load_sem, (feat_hbm, fx.at[own_rows, :]), (w_hbm, weight), (refresh_hbm, refresh)
+    )
     ready = me.greet()
-    f = me.feat
-    spread_to = lax.broadcasted_iota(I32, (64, TILE), 1)
-    spread_from = lax.broadcasted_iota(I32, (64, TILE), 0)
-    spread = (spread_to == spread_from + f * 64).astype(F32).astype(BF16)
-    wide[...] = dot(feat_ref[...], spread).astype(BF16)
-    chosen = rows_by_refresh(refresh_ref[pl.ds(me.dom, 1), :])
-    pick[...] = dot(chosen, wide[...]).astype(BF16)
+    loads[2].wait()
+    chosen = refresh_by_rows(refresh[pl.ds(me.dom, 1), :])
+    loads[0].wait()
+    pick[own_rows, :] = dot(fx[own_rows, :], chosen).astype(BF16)
+    loads[1].wait()
+    wcol[own_rows, :] = weight[:, own_columns]
     ready()
 
     def to_pair(k, src, dst):
@@ -132,16 +153,12 @@
             device_id_type=MESH,
         )
 
-    own_columns = pl.ds(pl.multiple_of(f * TILE, TILE), TILE)
-    pair_columns = pl.ds(pl.multiple_of((1 - f) * TILE, TILE), TILE)
-    own_rows = pl.ds(pl.multiple_of(f * 64, 64), 64)
-    pick_copy = to_pair(0, pick, pick_in)
+    pick_copy = to_pair(0, pick.at[own_rows, :], pick.at[own_rows, :])
     pick_copy.start()
-    w_copy = to_pair(1, w_ref.at[:, pair_columns], wcol.at[own_rows, :])
+    w_copy = to_pair(1, weight.at[:, pair_columns], wcol.at[own_rows, :])
     w_copy.start()
-    wide_copy = to_pair(2, wide, wide_in)
-    wide_copy.start()
-    wcol_out[own_rows, :] = w_ref[:, own_columns]
+    fx_copy = to_pair(2, fx.at[own_rows, :], fx.at[own_rows, :])
+    fx_copy.start()
 
     sends = []
 
@@ -170,7 +187,7 @@
     a, b, z, o = me.a, me.b, me.z, 1 - me.z
     mine = me.slot(a, b, z)
     pick_copy.wait_recv()
-    arr[pl.ds(mine, 1)] = (pick[...] + pick_in[...])[None]
+    arr[pl.ds(mine, 1)] = jnp.transpose(pick[...].astype(F32)).astype(BF16)[None]
 
     def spread_b(slot):
         send(slot, me.b_next)
@@ -249,12 +266,12 @@
 
     keep_own = keep(0, me.core * CLASS)
     keep_own.start()
-    wide_copy.wait_recv()
-    fx_out[...] = wide[...] + wide_in[...]
     w_copy.wait_recv()
-    wcol_out[pl.ds(pl.multiple_of((1 - f) * 64, 64), 64), :] = wcol[
-        pl.ds(pl.multiple_of((1 - f) * 64, 64), 64), :
-    ]
+    keep_w = pltpu.make_async_copy(wcol, wcol_out, out_sem.at[2])
+    keep_w.start()
+    fx_copy.wait_recv()
+    keep_fx = pltpu.make_async_copy(fx, fx_out, out_sem.at[3])
+    keep_fx.start()
     other = (1 - me.core) * CLASS
     for k in range(CLASS):
         arrive(other + k)
@@ -264,25 +281,28 @@
         copy.wait_send()
     pick_copy.wait_send()
     w_copy.wait_send()
-    wide_copy.wait_send()
+    fx_copy.wait_send()
     keep_own.wait()
     keep_other.wait()
+    keep_w.wait()
+    keep_fx.wait()
 
 
 CHUNK = 12
-AHEAD = 10
-UNROLL = 8
+GROUP = 8
+AHEAD = 2
+F_UNROLL = 64
 
 
 def forward_kernel(
     src_ref,
     dst_ref,
     count_ref,
-    refresh_ref,
-    fx_ref,
-    wcol_ref,
-    mask_ref,
-    gh_ref,
+    refresh_hbm,
+    fx_hbm,
+    wcol_hbm,
+    mask_hbm,
+    gh_hbm,
     arr_hbm,
     stale_hbm,
     tiles_hbm,
@@ -291,59 +311,90 @@
     source,
     tiles,
     arr,
+    fresh,
     acc,
+    refresh,
+    fx,
+    wcol,
+    mask,
+    gh,
     stale_sem,
     arr_sem,
     tile_sem,
+    load_sem,
 ):
     me = lax.axis_index("dom")
     live = count_ref[0]
+    groups = PARTS // GROUP
 
     def stale_copy(slot):
         rows = pl.ds(pl.multiple_of(slot_part(slot) * ROWS, ROWS), ROWS)
         return pltpu.make_async_copy(stale_hbm.at[rows], source.at[rows], stale_sem.at[slot])
 
-    def arr_copy(slot):
-        return pltpu.make_async_copy(arr_hbm.at[slot], arr.at[slot], arr_sem.at[slot])
+    def arr_copy(group):
+        part = pl.ds(group * GROUP, GROUP)
+        return pltpu.make_async_copy(arr_hbm.at[part], arr.at[part], arr_sem.at[group])
 
     def tile_copy(chunk):
         part = pl.ds(chunk * CHUNK, CHUNK)
         return pltpu.make_async_copy(tiles_hbm.at[part], tiles.at[part], tile_sem.at[chunk])
 
-    def first(slot, carry):
-        stale_copy(slot).start()
-        arr_copy(slot).start()
+    def start_group(group):
+        arr_copy(group).start()
+        for k in range(GROUP):
+            stale_copy(group * GROUP + k).start()
+
+    loads = fetch(load_sem, (wcol_hbm, wcol), (refresh_hbm, refresh))
+    for group in range(AHEAD):
+        start_group(group)
+    late = fetch(load_sem.at[pl.ds(2, 3)], (fx_hbm, fx), (mask_hbm, mask), (gh_hbm, gh))
+    acc[...] = jnp.zeros_like(acc)
+    ones = jnp.ones((REF, TILE), BF16)
+
+    def make_fresh(group):
+        rows = arr[pl.ds(group * GROUP, GROUP)].reshape(GROUP * REF, TILE)
+        fresh[group % 2] = dot(rows, wcol[...]).astype(BF16)
+
+    for copy in loads:
+        copy.wait()
+    arr_copy(0).wait()
+    make_fresh(0)
+
+    def merge(group, carry):
+        @pl.when(group + AHEAD < groups)
+        def _():
+            start_group(group + AHEAD)
+
+        for k in range(GROUP):
+
+            @pl.when((group * GROUP + k) * CHUNK < live)
+            def _():
+                tile_copy(group * GROUP + k).start()
+
+        @pl.when(group + 1 < groups)
+        def _():
+            arr_copy(group + 1).wait()
+
+        for k in range(GROUP):
+            stale_copy(group * GROUP + k).wait()
+        make_fresh(jnp.minimum(group + 1, groups - 1))
+        for k in range(GROUP):
+            part = slot_part(group * GROUP + k)
+            chosen = refresh_by_rows(refresh[pl.ds(part, 1), :])
+            new = fresh[group % 2, pl.ds(k * REF, REF), :]
+            placed = dot(chosen, jnp.concatenate([new, ones], axis=1))
+            rows = pl.ds(pl.multiple_of(part * ROWS, ROWS), ROWS)
+            old = source[rows, :].astype(F32)
+            source[rows, :] = jnp.where(placed[:, TILE:] > 0, placed[:, :TILE], old).astype(BF16)
         return carry
 
-    lax.fori_loop(0, AHEAD, first, 0)
-    acc[...] = jnp.zeros_like(acc)
-    wcol = wcol_ref[...]
-    ones = jnp.ones((REF, TILE), BF16)
-
-    def merge(slot, carry):
-        @pl.when(slot + AHEAD < PARTS)
-        def _():
-            stale_copy(slot + AHEAD).start()
-            arr_copy(slot + AHEAD).start()
-
-        @pl.when(slot * CHUNK < live)
-        def _():
-            tile_copy(slot).start()
-
-        part = slot_part(slot)
-        arr_copy(slot).wait()
-        fresh = dot(arr[pl.ds(slot, 1)][0], wcol).astype(BF16)
-        chosen = refresh_by_rows(refresh_ref[pl.ds(part, 1), :])
-        placed = dot(chosen, jnp.concatenate([fresh, ones], axis=1))
-        stale_copy(slot).wait()
-        rows = pl.ds(pl.multiple_of(part * ROWS, ROWS), ROWS)
-        old = source[rows, :].astype(F32)
-        source[rows, :] = jnp.where(placed[:, TILE:] > 0, placed[:, :TILE], old).astype(BF16)
-        return carry
-
-    lax.fori_loop(0, PARTS, merge, 0)
+    lax.fori_loop(0, groups, merge, 0)
+    for copy in late:
+        copy.wait()
     own = pl.ds(pl.multiple_of(me * ROWS, ROWS), ROWS)
-    source[own, :] = dot(fx_ref[...], wcol).astype(BF16)
+    source[own, :] = lax.dot_general(
+        fx[...], wcol[...], (((0,), (0,)), ((), ())), preferred_element_type=F32
+    ).astype(BF16)
 
     def wait_chunk(chunk, carry):
         tile_copy(chunk).wait()
@@ -352,48 +403,53 @@
     lax.fori_loop(0, (live + CHUNK - 1) // CHUNK, wait_chunk, 0)
 
     def step(index, carry):
-        for k in range(UNROLL):
-            t = index * UNROLL + k
+        for k in range(F_UNROLL):
+            t = index * F_UNROLL + k
             rows = pl.ds(pl.multiple_of(src_ref[t] * TILE, TILE), TILE)
             product = dot(tiles[t], source[rows, :])
             d = jnp.where(t < live, dst_ref[t], PER)
             acc[pl.ds(d, 1)] = acc[pl.ds(d, 1)] + product[None]
         return carry
 
-    lax.fori_loop(0, (live + UNROLL - 1) // UNROLL, step, 0)
+    lax.fori_loop(0, (live + F_UNROLL - 1) // F_UNROLL, step, 0)
 
     for d in range(PER):
         pre = acc[d]
         rows = pl.ds(d * TILE, TILE)
         hidden_ref[rows, :] = jnp.maximum(pre, 0.0).astype(BF16)
-        passed = jnp.where(pre > 0, gh_ref[rows, :].astype(F32), 0.0)
-        kept = mask_ref[pl.ds(d, 1), :].astype(F32)
+        passed = jnp.where(pre > 0, gh[rows, :].astype(F32), 0.0)
+        kept = mask[pl.ds(d, 1), :].astype(F32)
         delta_ref[d] = (jnp.transpose(passed) * kept).astype(BF16)
 
 
-B_CHUNK = 32
+B_CHUNK = 64
 B_RING = 4
+B_UNROLL = 64
 
 
 def backward_kernel(
     src_ref,
     dst_ref,
     count_ref,
-    refresh_ref,
-    fx_ref,
-    delta_ref,
+    refresh_hbm,
+    fx_hbm,
+    delta_hbm,
     arr_hbm,
     tiles_hbm,
     picked_hbm,
     own_ref,
     gw_ref,
     acc,
+    refresh,
+    fx,
+    delta,
     tiles,
     arr,
     picked,
     gw_total,
     tile_sem,
     arr_sem,
+    load_sem,
     out_sem,
 ):
     me = lax.axis_index("dom")
@@ -411,14 +467,18 @@
         def _():
             tile_copy(k).start()
 
+    loads = fetch(load_sem, (delta_hbm, delta), (refresh_hbm, refresh), (fx_hbm, fx))
     arr_copy = pltpu.make_async_copy(arr_hbm, arr, arr_sem)
     arr_copy.start()
 
-    def clear(block, carry):
-        acc[pl.ds(block, 1)] = jnp.zeros((1, TILE, TILE), F32)
+    def clear(index, carry):
+        acc[pl.ds(index * PER, PER)] = jnp.zeros((PER, TILE, TILE), F32)
         return carry
 
-    lax.fori_loop(0, BLOCKS + 1, clear, 0)
+    lax.fori_loop(0, BLOCKS // PER, clear, 0)
+    acc[BLOCKS] = jnp.zeros((TILE, TILE), F32)
+    for copy in loads:
+        copy.wait()
 
     def take_chunk(chunk, carry):
         @pl.when(chunk + B_RING - 1 < chunks)
@@ -429,15 +489,15 @@
         place = chunk % B_RING
 
         def step(index, carry):
-            for k in range(UNROLL):
-                local = index * UNROLL + k
+            for k in range(B_UNROLL):
+                local = index * B_UNROLL + k
                 t = chunk * B_CHUNK + local
-                product = dot(delta_ref[dst_ref[t]], tiles[place, local])
+                product = dot(delta[dst_ref[t]], tiles[place, local])
                 s = jnp.where(t < live, src_ref[t], BLOCKS)
                 acc[pl.ds(s, 1)] = acc[pl.ds(s, 1)] + product[None]
             return carry
 
-        return lax.fori_loop(0, B_CHUNK // UNROLL, step, carry)
+        return lax.fori_loop(0, B_CHUNK // B_UNROLL, step, carry)
 
     lax.fori_loop(0, chunks, take_chunk, 0)
     arr_copy.wait()
@@ -446,21 +506,27 @@
     def out_copy(slot):
         return pltpu.make_async_copy(picked.at[slot], picked_hbm.at[slot], out_sem.at[slot])
 
-    def pick(slot, carry):
-        part = slot_part(slot)
-        chosen = refresh_by_rows(refresh_ref[pl.ds(part, 1), :])
-        blocks = [acc[part * PER + k].astype(BF16) for k in range(PER)]
-        grads = dot(jnp.concatenate(blocks, axis=1), chosen)
-        grads = jnp.where(part == me, 0.0, grads).astype(BF16)
-        picked[pl.ds(slot, 1)] = grads[None]
-        out_copy(slot).start()
-        gw_total[...] += dot(grads, arr[pl.ds(slot, 1)][0])
+    def pick(group, carry):
+        total = gw_total[...]
+        for k in range(GROUP):
+            slot = group * GROUP + k
+            part = slot_part(slot)
+            chosen = refresh_by_rows(refresh[pl.ds(part, 1), :])
+            blocks = [acc[part * PER + i].astype(BF16) for i in range(PER)]
+            grads = dot(jnp.concatenate(blocks, axis=1), chosen)
+            grads = jnp.where(part == me, 0.0, grads).astype(BF16)
+            picked[pl.ds(slot, 1)] = grads[None]
+            out_copy(slot).start()
+            total = total + dot(grads, arr[pl.ds(slot, 1)][0])
+        gw_total[...] = total
         return carry
 
-    lax.fori_loop(0, PARTS, pick, 0)
+    lax.fori_loop(0, PARTS // GROUP, pick, 0)
     for k in range(PER):
         own_ref[:, pl.ds(k * TILE, TILE)] = acc[me * PER + k]
-    gw = gw_total[...] + dot(own_ref[...].astype(BF16), fx_ref[...])
+    gw = gw_total[...] + lax.dot_general(
+        own_ref[...].astype(BF16), fx[...], (((1,), (1,)), ((), ())), preferred_element_type=F32
+    )
     gw_ref[...] = jnp.transpose(gw)
 
     def wait_out(slot, carry):
@@ -471,13 +537,16 @@
 
 
 def scatter_kernel(
-    refresh_ref,
-    w_ref,
-    own_ref,
-    gw_ref,
+    refresh_hbm,
+    w_hbm,
+    own_hbm,
+    gw_hbm,
     picked_hbm,
     gf_out,
     gw_out,
+    refresh,
+    weight,
+    own,
     work,
     sib,
     from_b1,
@@ -491,11 +560,15 @@
     grad,
     grad_in,
     load_sem,
+    small_sem,
     send_sem,
     recv_sem,
 ):
     me = Place()
     ready = me.greet()
+    small = fetch(
+        small_sem, (gw_hbm, sums.at[0]), (own_hbm, own), (w_hbm, weight), (refresh_hbm, refresh)
+    )
     f, a, b, z = me.feat, me.a, me.b, me.z
     loads = []
     for k, chunk in enumerate((b + 2, b + 1, b + 3, b)):
@@ -507,7 +580,7 @@
         )
         copy.start()
         loads.append(copy)
-    sums[0] = gw_ref[...]
+    small[0].wait()
     ready()
     sends = []
 
@@ -601,7 +674,9 @@
     a1_down.wait_recv()
     add(work, down + 1, 1, from_a1[pl.ds(1, 1)])
     a2_down_late = send(work.at[pl.ds(down + 1, 1)], from_a2.at[1, pl.ds(1, 1)], me.a_prev)
-    chosen = rows_by_refresh(refresh_ref[pl.ds(me.dom, 1), :])
+    for copy in small[1:]:
+        copy.wait()
+    chosen = rows_by_refresh(refresh[pl.ds(me.dom, 1), :])
     sum_take(4, gw_copy)
     gw_copy = sum_send(5)
     a2_up_late.wait_recv()
@@ -616,17 +691,17 @@
     swap = send(sums.at[6, other_rows, :], gw_in, me.dom, 1 - f)
     z_copy.wait_recv()
     carried = work[pl.ds(mine + z, 1)][0].astype(F32) + from_z[0].astype(F32)
-    grad[...] = (own_ref[...] + dot(carried.astype(BF16), chosen)).astype(BF16)
+    grad[...] = (own[...] + dot(carried.astype(BF16), chosen)).astype(BF16)
     grad_copy = send(grad, grad_in, me.dom, 1 - f)
     own_columns = pl.ds(pl.multiple_of(f * TILE, TILE), TILE)
     other_columns = pl.ds(pl.multiple_of((1 - f) * TILE, TILE), TILE)
-    half = dot(w_ref[:, own_columns], grad[...])
+    half = dot(weight[:, own_columns], grad[...])
     swap.wait_recv()
     gw_out[:, own_columns] = sums[6, own_rows, :]
     gw_out[:, other_columns] = gw_in[...]
     grad_copy.wait_recv()
-    half = half + dot(w_ref[:, other_columns], grad_in[...])
-    gf_out[...] = jnp.transpose(half).astype(BF16)
+    half = half + dot(weight[:, other_columns], grad_in[...])
+    gf_out[...] = half.astype(BF16)
     for copy in sends:
         copy.wait_send()
 
@@ -639,6 +714,133 @@
 
 def shape(dims, kind):
     return jax.ShapeDtypeStruct(dims, kind)
+
+
+def scratch(dims, kind):
+    return pltpu.VMEM(dims, kind)
+
+
+def params(**fields):
+    return pltpu.CompilerParams(vmem_limit_bytes=62 * MIB, **fields)
+
+
+def call_gather(features, weight, refresh):
+    return pl.pallas_call(
+        gather_kernel,
+        out_shape=(
+            shape((PARTS, REF, TILE), BF16),
+            shape((TILE, ROWS), BF16),
+            shape((TILE, TILE), BF16),
+        ),
+        in_specs=[ANY] * 3,
+        out_specs=(ANY, ANY, ANY),
+        scratch_shapes=[
+            scratch((PARTS, REF, TILE), BF16),
+            scratch((TILE, REF), BF16),
+            scratch((TILE, ROWS), BF16),
+            scratch((64, 2 * TILE), BF16),
+            scratch((TILE, TILE), BF16),
+            scratch((PARTS, REF), I32),
+            DMA((63,)),
+            DMA((PARTS,)),
+            DMA((3,)),
+            DMA((3,)),
+            DMA((3,)),
+            DMA((4,)),
+        ],
+        compiler_params=params(collective_id=0, has_side_effects=True),
+        name="gather_refreshed",
+    )(features, weight, refresh)
+
+
+def call_forward(
+    src, dst, count, refresh, fx, wcol, mask, gh, arr, stale, tiles, name="forward_tiles"
+):
+    return pl.pallas_call(
+        forward_kernel,
+        out_shape=(shape((ROWS, TILE), BF16), shape((PER, TILE, TILE), BF16)),
+        in_specs=[SMEM] * 3 + [ANY] * 8,
+        out_specs=(VMEM, VMEM),
+        scratch_shapes=[
+            scratch((PARTS * ROWS, TILE), BF16),
+            scratch((NT, TILE, TILE), BF16),
+            scratch((PARTS, REF, TILE), BF16),
+            scratch((2, GROUP * REF, TILE), BF16),
+            scratch((PER + 1, TILE, TILE), F32),
+            scratch((PARTS, REF), I32),
+            scratch((TILE, ROWS), BF16),
+            scratch((TILE, TILE), BF16),
+            scratch((PER, TILE), I32),
+            scratch((ROWS, TILE), BF16),
+            DMA((PARTS,)),
+            DMA((PARTS // GROUP,)),
+            DMA((NT // CHUNK,)),
+            DMA((5,)),
+        ],
+        compiler_params=params(),
+        name=name,
+    )(src, dst, count, refresh, fx, wcol, mask, gh, arr, stale, tiles)
+
+
+def call_backward(src, dst, count, refresh, fx, delta, arr, tiles, name="backward_tiles"):
+    return pl.pallas_call(
+        backward_kernel,
+        out_shape=(
+            shape((PARTS, TILE, REF), BF16),
+            shape((TILE, ROWS), F32),
+            shape((TILE, TILE), F32),
+        ),
+        in_specs=[SMEM] * 3 + [ANY] * 5,
+        out_specs=(ANY, VMEM, VMEM),
+        scratch_shapes=[
+            scratch((BLOCKS + 1, TILE, TILE), F32),
+            scratch((PARTS, REF), I32),
+            scratch((TILE, ROWS), BF16),
+            scratch((PER, TILE, TILE), BF16),
+            scratch((B_RING, B_CHUNK, TILE, TILE), BF16),
+            scratch((PARTS, REF, TILE), BF16),
+            scratch((PARTS, TILE, REF), BF16),
+            scratch((TILE, TILE), F32),
+            DMA((B_RING,)),
+            DMA,
+            DMA((3,)),
+            DMA((PARTS,)),
+        ],
+        compiler_params=params(),
+        name=name,
+    )(src, dst, count, refresh, fx, delta, arr, tiles)
+
+
+def call_scatter(refresh, weight, own, gw, picked):
+    return pl.pallas_call(
+        scatter_kernel,
+        out_shape=(shape((64, ROWS), BF16), shape((64, 2 * TILE), F32)),
+        in_specs=[ANY] * 5,
+        out_specs=(VMEM, VMEM),
+        scratch_shapes=[
+            scratch((PARTS, REF), I32),
+            scratch((64, 2 * TILE), BF16),
+            scratch((TILE, ROWS), F32),
+            scratch((CLASS, TILE, REF), BF16),
+            scratch((CLASS, TILE, REF), BF16),
+            scratch((8, TILE, REF), BF16),
+            scratch((2, 8, TILE, REF), BF16),
+            scratch((2, TILE, REF), BF16),
+            scratch((2, 2, TILE, REF), BF16),
+            scratch((1, TILE, REF), BF16),
+            scratch((7, TILE, TILE), F32),
+            scratch((6, TILE, TILE), F32),
+            scratch((64, TILE), F32),
+            scratch((TILE, ROWS), BF16),
+            scratch((TILE, ROWS), BF16),
+            DMA((4,)),
+            DMA((4,)),
+            DMA((32,)),
+            DMA((32,)),
+        ],
+        compiler_params=params(collective_id=1, has_side_effects=True),
+        name="scatter_gradients",
+    )(refresh, weight, own, gw, picked)
 
 
 def shards(
@@ -653,112 +855,26 @@
     train_mask,
     grad_hidden,
 ):
-    arr, fx, wcol = pl.pallas_call(
-        gather_kernel,
-        out_shape=(
-            shape((PARTS, REF, TILE), BF16),
-            shape((ROWS, TILE), BF16),
-            shape((TILE, TILE), BF16),
-        ),
-        in_specs=[VMEM, VMEM, VMEM],
-        out_specs=(ANY, VMEM, VMEM),
-        scratch_shapes=[
-            pltpu.VMEM((PARTS, REF, TILE), BF16),
-            pltpu.VMEM((REF, TILE), BF16),
-            pltpu.VMEM((REF, TILE), BF16),
-            pltpu.VMEM((ROWS, TILE), BF16),
-            pltpu.VMEM((ROWS, TILE), BF16),
-            pltpu.VMEM((TILE, TILE), BF16),
-            DMA((63,)),
-            DMA((PARTS,)),
-            DMA((3,)),
-            DMA((3,)),
-            DMA((2,)),
-        ],
-        compiler_params=pltpu.CompilerParams(
-            collective_id=0, has_side_effects=True, vmem_limit_bytes=32 * MIB
-        ),
-        name="gather_refreshed",
-    )(features, weight, refresh)
-    hidden, delta = pl.pallas_call(
-        forward_kernel,
-        out_shape=(shape((ROWS, TILE), BF16), shape((PER, TILE, TILE), BF16)),
-        in_specs=[SMEM, SMEM, SMEM, VMEM, VMEM, VMEM, VMEM, VMEM, ANY, ANY, ANY],
-        out_specs=(VMEM, VMEM),
-        scratch_shapes=[
-            pltpu.VMEM((PARTS * ROWS, TILE), BF16),
-            pltpu.VMEM((NT, TILE, TILE), BF16),
-            pltpu.VMEM((PARTS, REF, TILE), BF16),
-            pltpu.VMEM((PER + 1, TILE, TILE), F32),
-            DMA((PARTS,)),
-            DMA((PARTS,)),
-            DMA((NT // CHUNK,)),
-        ],
-        compiler_params=pltpu.CompilerParams(vmem_limit_bytes=60 * MIB),
-        name="forward_tiles",
-    )(
+    arr, fx, wcol = call_gather(features.T, weight, refresh)
+    mask = train_mask.reshape(PER, TILE)
+    hidden, delta = call_forward(
         tile_src,
         tile_dst,
         tile_count,
         refresh,
         fx,
         wcol,
-        train_mask.reshape(PER, TILE),
+        mask,
         grad_hidden,
         arr,
         stale_cache,
         adj_tiles,
     )
-    picked, own, gw = pl.pallas_call(
-        backward_kernel,
-        out_shape=(
-            shape((PARTS, TILE, REF), BF16),
-            shape((TILE, ROWS), F32),
-            shape((TILE, TILE), F32),
-        ),
-        in_specs=[SMEM, SMEM, SMEM, VMEM, VMEM, VMEM, ANY, ANY],
-        out_specs=(ANY, VMEM, VMEM),
-        scratch_shapes=[
-            pltpu.VMEM((BLOCKS + 1, TILE, TILE), F32),
-            pltpu.VMEM((B_RING, B_CHUNK, TILE, TILE), BF16),
-            pltpu.VMEM((PARTS, REF, TILE), BF16),
-            pltpu.VMEM((PARTS, TILE, REF), BF16),
-            pltpu.VMEM((TILE, TILE), F32),
-            DMA((B_RING,)),
-            DMA,
-            DMA((PARTS,)),
-        ],
-        compiler_params=pltpu.CompilerParams(vmem_limit_bytes=60 * MIB),
-        name="backward_tiles",
-    )(tile_src, tile_dst, tile_count, refresh, fx, delta, arr, adj_tiles)
-    grad_features, grad_weight = pl.pallas_call(
-        scatter_kernel,
-        out_shape=(shape((ROWS, 64), BF16), shape((64, 2 * TILE), F32)),
-        in_specs=[VMEM, VMEM, VMEM, VMEM, ANY],
-        out_specs=(VMEM, VMEM),
-        scratch_shapes=[
-            pltpu.VMEM((CLASS, TILE, REF), BF16),
-            pltpu.VMEM((CLASS, TILE, REF), BF16),
-            pltpu.VMEM((8, TILE, REF), BF16),
-            pltpu.VMEM((2, 8, TILE, REF), BF16),
-            pltpu.VMEM((2, TILE, REF), BF16),
-            pltpu.VMEM((2, 2, TILE, REF), BF16),
-            pltpu.VMEM((1, TILE, REF), BF16),
-            pltpu.VMEM((7, TILE, TILE), F32),
-            pltpu.VMEM((6, TILE, TILE), F32),
-            pltpu.VMEM((64, TILE), F32),
-            pltpu.VMEM((TILE, ROWS), BF16),
-            pltpu.VMEM((TILE, ROWS), BF16),
-            DMA((4,)),
-            DMA((32,)),
-            DMA((32,)),
-        ],
-        compiler_params=pltpu.CompilerParams(
-            collective_id=1, has_side_effects=True, vmem_limit_bytes=32 * MIB
-        ),
-        name="scatter_gradients",
-    )(refresh, weight, own, gw, picked)
-    return hidden, grad_features, grad_weight
+    picked, own, gw = call_backward(
+        tile_src, tile_dst, tile_count, refresh, fx, delta, arr, adj_tiles
+    )
+    grad_features, grad_weight = call_scatter(refresh, weight, own, gw, picked)
+    return hidden, grad_features.T, grad_weight
 
 
 def solution(mesh):

time: 201 us -> 142 us (0.71)
  Pallas kernels: 187 us -> 136 us
  local copies, waits for them, and re-layouts: 11.4 us -> 3.04 us
    pallas_call x4, Pallas kernels: 187 us -> 136 us  [the longest x1 47.3 us: call_scatter(): pl.pallas_call(scatter_kernel, out_shape=(shape((64, ROWS), BF16), shape(...]
    unnamed x23 -> x2, local copies, waits for them, and re-layouts: 11.4 us -> 3.04 us
where the time goes in v2:
time: 142 us; the launch traced here: 140 us
  Pallas kernels  136 us (96%)
  local copies, waits for them, and re-layouts  3.04 us (2%)
    pallas_call x1, Pallas kernels, call_scatter(): pl.pallas_call(scatter_kernel, out_shape=(shape((64, ROWS), BF16), shape(...  47.3 us
    pallas_call x1, Pallas kernels, call_gather(): pl.pallas_call(gather_kernel, out_shape=(shape((PARTS, REF, TILE), BF16),...  32 us
    pallas_call x1, Pallas kernels, call_forward(): pl.pallas_call(forward_kernel, out_shape=(shape((ROWS, TILE), BF16), shap...  29.1 us
    pallas_call x1, Pallas kernels, call_backward(): pl.pallas_call(backward_kernel, out_shape=(shape((PARTS, TILE, REF), BF16...  27.7 us
    unnamed x2, local copies, waits for them, and re-layouts  3.04 us

profile of v2, /device:TPU:0, one launch (start us, length us, event | category | flops | bytes accessed | tf_op | source)
XLA Modules:
  0.0 140.5 jit_solution(6245166128056284207)
XLA Ops:
  1.3 32.0 %gather_refreshed.1 = (bf16[64,256,128]{2,1,0:T(8,128)(2,1)}, bf16[128,1024]{1,0:T(8,128)(2,1)}, bf16[128,128]{1,0:T(8,128)(2,1)}) custom-call(bf16[64,1024]{1,0:T(8,128)(2,1)} %bitcast.3, bf16[64,256]{1,0:T(8,128)(2,1)} %w_hbm.3, s32[64,256]{1,0:T(8,128)} %refresh_hbm.7), custom_call_target="tpu_custom_call" | custom-call | tf_op jit(solution)/shard_map/gather_refreshed/pallas_call | solution.py:728
  33.3 29.1 %forward_tiles.1 = (bf16[1024,128]{1,0:T(8,128)(2,1)}, bf16[8,128,128]{2,1,0:T(8,128)(2,1)}) custom-call(s32[768]{0:T(1024)} %src_ref.3, s32[768]{0:T(1024)} %dst_ref.3, s32[1]{0:T(128)S(6)} %copy.15.count_ref, s32[64,256]{1,0:T(8,128)} %refresh_hbm.7, bf16[128,1024]{1,0:T(8,128)(2,1)} %get-tuple-element.13.fx_hbm, ...), custom_call_target="tpu_custom_call" | custom-call | tf_op jit(solution)/shard_map/forward_tiles/pallas_call | solution.py:759
  62.3 27.7 %backward_tiles.1 = (bf16[64,128,256]{2,1,0:T(8,128)(2,1)}, f32[128,1024]{1,0:T(8,128)}, f32[128,128]{1,0:T(8,128)}) custom-call(s32[768]{0:T(1024)} %src_ref.3, s32[768]{0:T(1024)} %dst_ref.3, s32[1]{0:T(128)S(6)} %copy.15.count_ref, s32[64,256]{1,0:T(8,128)} %refresh_hbm.7, bf16[128,1024]{1,0:T(8,128)(2,1)} %get-tuple-element.13.fx_hbm, ...), custom_call_target="tpu_custom_call" | custom-call | tf_op jit(solution)/shard_map/backward_tiles/pallas_call | solution.py:786
  90.1 47.3 %scatter_gradients.1 = (bf16[64,1024]{1,0:T(8,128)(2,1)}, f32[64,256]{1,0:T(8,128)}) custom-call(s32[64,256]{1,0:T(8,128)} %refresh_hbm.7, bf16[64,256]{1,0:T(8,128)(2,1)} %w_hbm.3, f32[128,1024]{1,0:T(8,128)} %get-tuple-element.18.own_hbm, f32[128,128]{1,0:T(8,128)} %get-tuple-element.19.gw_hbm, bf16[64,128,256]{2,1,0:T(8,128)(2,1)} %get-tuple-element.20.picked_hbm), custom_call_target="tpu_custom_call" | custom-call | tf_op jit(solution)/shard_map/scatter_gradients/pallas_call | solution.py:815
  137.4 1.6 %copy.16 = bf16[1024,64]{0,1:T(8,128)(2,1)} copy(bf16[1024,64]{0,1:T(8,128)(2,1)} %bitcast.4) | data formatting | bytes 262144
  139.0 1.5 %copy.17 = f32[64,256]{1,0:T(8,128)} copy(f32[64,256]{1,0:T(8,128)} %get-tuple-element.28) | data formatting | bytes 131072

commit v3 on v2

--- a/solution.py
+++ b/solution.py
@@ -42,6 +42,7 @@
         self.a_prev = self.at(self.a + 3, self.b)
         self.b_next = self.at(self.a, self.b + 1)
         self.b_prev = self.at(self.a, self.b + 3)
+        self.a_far = self.at(self.a + 2, self.b)
 
     def at(self, a, b):
         a, b = a % RING, b % RING
@@ -55,9 +56,10 @@
     def slot(self, a, b, z):
         return self.core * CLASS + (b % RING) * 8 + (a % RING) * 2 + z
 
-    def greet(self):
+    def greet(self, *more):
         barrier = pltpu.get_barrier_semaphore()
         near = (self.sibling, self.z_pair, self.a_next, self.a_prev, self.b_next, self.b_prev)
+        near = near + more
         for device in near:
             pl.semaphore_signal(barrier, inc=1, device_id=(device, self.feat), device_id_type=MESH)
         pl.semaphore_signal(
@@ -107,14 +109,21 @@
     return pl.ds(pl.multiple_of(index * TILE, TILE), TILE)
 
 
+def plane(p):
+    h = p // 2
+    return (1 - h // 2) * 3 * h + (h // 2) * (h - 1), p % 2
+
+
 def gather_kernel(
     feat_hbm,
     w_hbm,
     refresh_hbm,
+    stale_hbm,
     arr_out,
     fx_out,
-    wcol_out,
+    source_out,
     arr,
+    source,
     pick,
     fx,
     weight,
@@ -125,7 +134,9 @@
     pair_send,
     pair_recv,
     load_sem,
+    stale_sem,
     out_sem,
+    row_sem,
 ):
     me = Place()
     f = me.feat
@@ -134,7 +145,9 @@
     loads = fetch(
         load_sem, (feat_hbm, fx.at[own_rows, :]), (w_hbm, weight), (refresh_hbm, refresh)
     )
-    ready = me.greet()
+    stale_copy = pltpu.make_async_copy(stale_hbm, source, stale_sem)
+    stale_copy.start()
+    ready = me.greet(me.a_far)
     loads[2].wait()
     chosen = refresh_by_rows(refresh[pl.ds(me.dom, 1), :])
     loads[0].wait()
@@ -160,259 +173,217 @@
     fx_copy = to_pair(2, fx.at[own_rows, :], fx.at[own_rows, :])
     fx_copy.start()
 
-    sends = []
-
-    def send(slot, target):
-        copy = pltpu.make_async_remote_copy(
+    def shard(slot, target, kind, p):
+        return pltpu.make_async_remote_copy(
             src_ref=arr.at[slot],
             dst_ref=arr.at[slot],
-            send_sem=send_sem.at[len(sends)],
+            send_sem=send_sem.at[kind, p],
             recv_sem=recv_sem.at[slot],
             device_id=(target, f),
             device_id_type=MESH,
         )
-        copy.start()
-        sends.append(copy)
 
     def arrive(slot):
-        pltpu.make_async_remote_copy(
-            src_ref=arr.at[slot],
-            dst_ref=arr.at[slot],
-            send_sem=send_sem.at[0],
-            recv_sem=recv_sem.at[slot],
-            device_id=(me.sibling, f),
-            device_id_type=MESH,
-        ).wait_recv()
-
-    a, b, z, o = me.a, me.b, me.z, 1 - me.z
-    mine = me.slot(a, b, z)
+        shard(slot, me.sibling, 0, 0).wait_recv()
+
+    def slot_of(p, b_offset):
+        a_offset, pair = plane(p)
+        return me.slot(me.a + a_offset, me.b + b_offset, (me.z + pair) % 2)
+
+    def pass_on(p):
+        slot = slot_of(p, 0)
+        shard(slot, me.b_next, 0, p).start()
+        shard(slot, me.b_prev, 1, p).start()
+        shard(slot, me.sibling, 3, p).start()
+
+    def along_a(p):
+        slot = slot_of(p, 0)
+        shard(slot, me.a_next, 7, p).start()
+        shard(slot, me.a_prev, 8, p).start()
+        shard(slot, me.a_far, 9, p).start()
+
+    def take_plane(p):
+        slot = slot_of(p, 0)
+        arrive(slot)
+        return slot
+
+    def take_b(p):
+        below, above = slot_of(p, 3), slot_of(p, 1)
+        arrive(below)
+
+        @pl.when(p % 2 == 0)
+        def _():
+            shard(below, me.b_next, 2, p).start()
+
+        shard(below, me.sibling, 4, p).start()
+        arrive(above)
+
+        @pl.when(p % 2 == 1)
+        def _():
+            shard(above, me.b_prev, 2, p).start()
+
+        shard(above, me.sibling, 5, p).start()
+        return below, above
+
+    def take_far(p):
+        slot = slot_of(p, 2)
+        arrive(slot)
+        shard(slot, me.sibling, 6, p).start()
+        return slot
+
+    ones = jnp.ones((REF, TILE), BF16)
+
+    def rows_of(part):
+        return pl.ds(pl.multiple_of(part * ROWS, ROWS), ROWS)
+
+    def row_copy(part):
+        rows = rows_of(part)
+        return pltpu.make_async_copy(source.at[rows], source_out.at[rows], row_sem.at[part])
+
+    def merge(*slots):
+        fresh = [dot(arr[pl.ds(slot, 1)][0], wcol[...]).astype(BF16) for slot in slots]
+        for slot, new in zip(slots, fresh):
+            part = slot_part(slot)
+            chosen = refresh_by_rows(refresh[pl.ds(part, 1), :])
+            placed = dot(chosen, jnp.concatenate([new, ones], axis=1))
+            rows = rows_of(part)
+            old = source[rows, :].astype(F32)
+            source[rows, :] = jnp.where(placed[:, TILE:] > 0, placed[:, :TILE], old).astype(BF16)
+        for slot in slots:
+            row_copy(slot_part(slot)).start()
+
+    mine = slot_of(0, 0)
     pick_copy.wait_recv()
     arr[pl.ds(mine, 1)] = jnp.transpose(pick[...].astype(F32)).astype(BF16)[None]
-
-    def spread_b(slot):
-        send(slot, me.b_next)
-        send(slot, me.b_prev)
-        send(slot, me.sibling)
-
-    send(mine, me.z_pair)
-    send(mine, me.a_next)
-    send(mine, me.a_prev)
-    spread_b(mine)
-
-    slot = me.slot(a, b, o)
-    arrive(slot)
-    send(slot, me.a_next)
-    send(slot, me.a_prev)
-    spread_b(slot)
-
-    slot = me.slot(a + 3, b, z)
-    arrive(slot)
-    send(slot, me.a_next)
-    spread_b(slot)
-    slot = me.slot(a + 1, b, z)
-    arrive(slot)
-    spread_b(slot)
-
-    def ring_b(aa, zz):
-        slot = me.slot(aa, b + 3, zz)
-        arrive(slot)
-        if zz is z:
-            send(slot, me.b_next)
-        send(slot, me.sibling)
-        slot = me.slot(aa, b + 1, zz)
-        arrive(slot)
-        if zz is not z:
-            send(slot, me.b_prev)
-        send(slot, me.sibling)
-
-    ring_b(a, z)
-    slot = me.slot(a + 3, b, o)
-    arrive(slot)
-    spread_b(slot)
-    slot = me.slot(a + 1, b, o)
-    arrive(slot)
-    send(slot, me.a_prev)
-    spread_b(slot)
-    ring_b(a, o)
-    slot = me.slot(a + 2, b, z)
-    arrive(slot)
-    spread_b(slot)
-    slot = me.slot(a + 2, b, o)
-    arrive(slot)
-    spread_b(slot)
-    ring_b(a + 3, z)
-    ring_b(a + 1, z)
-    ring_b(a + 3, o)
-    ring_b(a + 1, o)
-    ring_b(a + 2, z)
-    ring_b(a + 2, o)
-    for aa, zz in (
-        (a, z),
-        (a, o),
-        (a + 3, z),
-        (a + 1, z),
-        (a + 3, o),
-        (a + 1, o),
-        (a + 2, z),
-        (a + 2, o),
-    ):
-        slot = me.slot(aa, b + 2, zz)
-        arrive(slot)
-        send(slot, me.sibling)
-
-    def keep(k, first):
-        part = pl.ds(first, CLASS)
-        return pltpu.make_async_copy(arr.at[part], arr_out.at[part], out_sem.at[k])
-
-    keep_own = keep(0, me.core * CLASS)
+    pair_sent = shard(mine, me.z_pair, 2, PER)
+    pair_sent.start()
+    along_a(0)
+    pass_on(0)
+    first = take_plane(1)
+    along_a(1)
+    pass_on(1)
+    below, above = take_b(0)
+    w_copy.wait_recv()
+    stale_copy.wait()
+    merge(first, below, above)
+
+    def relay(i, carry):
+        near = take_plane(i + 1)
+        pass_on(i + 1)
+        below, above = take_b(i)
+        far = take_far(i - 1)
+        merge(near, below, above, far)
+        return carry
+
+    lax.fori_loop(1, PER - 1, relay, 0)
+    below, above = take_b(PER - 1)
+    far = take_far(PER - 2)
+    last = take_far(PER - 1)
+    own_class = pl.ds(me.core * CLASS, CLASS)
+    keep_own = pltpu.make_async_copy(arr.at[own_class], arr_out.at[own_class], out_sem.at[0])
     keep_own.start()
-    w_copy.wait_recv()
-    keep_w = pltpu.make_async_copy(wcol, wcol_out, out_sem.at[2])
-    keep_w.start()
+    merge(below, above, far, last)
     fx_copy.wait_recv()
-    keep_fx = pltpu.make_async_copy(fx, fx_out, out_sem.at[3])
+    keep_fx = pltpu.make_async_copy(fx, fx_out, out_sem.at[2])
     keep_fx.start()
-    other = (1 - me.core) * CLASS
-    for k in range(CLASS):
-        arrive(other + k)
-    keep_other = keep(1, other)
+    source[rows_of(me.dom), :] = lax.dot_general(
+        fx[...], wcol[...], (((0,), (0,)), ((), ())), preferred_element_type=F32
+    ).astype(BF16)
+    row_copy(me.dom).start()
+
+    def take_sibling(p, carry):
+        a_offset, pair = plane(p)
+        a, z = (me.b + a_offset) % RING, (me.z + pair) % 2
+        first = (1 - me.core) * CLASS + a * 2 + z
+        slots = [first + ((me.a + offset) % RING) * 8 for offset in (0, 3, 1, 2)]
+        for slot in slots:
+            arrive(slot)
+        merge(*slots)
+        return carry
+
+    lax.fori_loop(0, PER, take_sibling, 0)
+    other_class = pl.ds((1 - me.core) * CLASS, CLASS)
+    keep_other = pltpu.make_async_copy(arr.at[other_class], arr_out.at[other_class], out_sem.at[1])
     keep_other.start()
-    for copy in sends:
-        copy.wait_send()
+
+    def settle(p, carry):
+        for kind in range(7):
+            shard(mine, me.sibling, kind, p).wait_send()
+        return carry
+
+    lax.fori_loop(0, PER, settle, 0)
+    for p in range(2):
+        for kind in range(7, 10):
+            shard(mine, me.sibling, kind, p).wait_send()
+    pair_sent.wait_send()
     pick_copy.wait_send()
     w_copy.wait_send()
     fx_copy.wait_send()
+
+    def settle_rows(part, carry):
+        row_copy(part).wait()
+        return carry
+
+    lax.fori_loop(0, PARTS, settle_rows, 0)
     keep_own.wait()
+    keep_fx.wait()
     keep_other.wait()
-    keep_w.wait()
-    keep_fx.wait()
-
-
-CHUNK = 12
+
+
 GROUP = 8
-AHEAD = 2
-F_UNROLL = 64
+CHUNK = 64
 
 
 def forward_kernel(
     src_ref,
     dst_ref,
     count_ref,
-    refresh_hbm,
-    fx_hbm,
-    wcol_hbm,
     mask_hbm,
     gh_hbm,
-    arr_hbm,
-    stale_hbm,
+    source_hbm,
     tiles_hbm,
     hidden_ref,
     delta_ref,
     source,
     tiles,
-    arr,
-    fresh,
     acc,
-    refresh,
-    fx,
-    wcol,
     mask,
     gh,
-    stale_sem,
-    arr_sem,
+    source_sem,
     tile_sem,
     load_sem,
 ):
-    me = lax.axis_index("dom")
     live = count_ref[0]
-    groups = PARTS // GROUP
-
-    def stale_copy(slot):
-        rows = pl.ds(pl.multiple_of(slot_part(slot) * ROWS, ROWS), ROWS)
-        return pltpu.make_async_copy(stale_hbm.at[rows], source.at[rows], stale_sem.at[slot])
-
-    def arr_copy(group):
-        part = pl.ds(group * GROUP, GROUP)
-        return pltpu.make_async_copy(arr_hbm.at[part], arr.at[part], arr_sem.at[group])
+    chunks = (live + CHUNK - 1) // CHUNK
+    source_copy = pltpu.make_async_copy(source_hbm, source, source_sem)
+    source_copy.start()
 
     def tile_copy(chunk):
         part = pl.ds(chunk * CHUNK, CHUNK)
         return pltpu.make_async_copy(tiles_hbm.at[part], tiles.at[part], tile_sem.at[chunk])
 
-    def start_group(group):
-        arr_copy(group).start()
-        for k in range(GROUP):
-            stale_copy(group * GROUP + k).start()
-
-    loads = fetch(load_sem, (wcol_hbm, wcol), (refresh_hbm, refresh))
-    for group in range(AHEAD):
-        start_group(group)
-    late = fetch(load_sem.at[pl.ds(2, 3)], (fx_hbm, fx), (mask_hbm, mask), (gh_hbm, gh))
+    def start_chunk(chunk, carry):
+        tile_copy(chunk).start()
+        return carry
+
+    lax.fori_loop(0, chunks, start_chunk, 0)
+    late = fetch(load_sem, (mask_hbm, mask), (gh_hbm, gh))
     acc[...] = jnp.zeros_like(acc)
-    ones = jnp.ones((REF, TILE), BF16)
-
-    def make_fresh(group):
-        rows = arr[pl.ds(group * GROUP, GROUP)].reshape(GROUP * REF, TILE)
-        fresh[group % 2] = dot(rows, wcol[...]).astype(BF16)
-
-    for copy in loads:
-        copy.wait()
-    arr_copy(0).wait()
-    make_fresh(0)
-
-    def merge(group, carry):
-        @pl.when(group + AHEAD < groups)
-        def _():
-            start_group(group + AHEAD)
-
-        for k in range(GROUP):
-
-            @pl.when((group * GROUP + k) * CHUNK < live)
-            def _():
-                tile_copy(group * GROUP + k).start()
-
-        @pl.when(group + 1 < groups)
-        def _():
-            arr_copy(group + 1).wait()
-
-        for k in range(GROUP):
-            stale_copy(group * GROUP + k).wait()
-        make_fresh(jnp.minimum(group + 1, groups - 1))
-        for k in range(GROUP):
-            part = slot_part(group * GROUP + k)
-            chosen = refresh_by_rows(refresh[pl.ds(part, 1), :])
-            new = fresh[group % 2, pl.ds(k * REF, REF), :]
-            placed = dot(chosen, jnp.concatenate([new, ones], axis=1))
-            rows = pl.ds(pl.multiple_of(part * ROWS, ROWS), ROWS)
-            old = source[rows, :].astype(F32)
-            source[rows, :] = jnp.where(placed[:, TILE:] > 0, placed[:, :TILE], old).astype(BF16)
-        return carry
-
-    lax.fori_loop(0, groups, merge, 0)
-    for copy in late:
-        copy.wait()
-    own = pl.ds(pl.multiple_of(me * ROWS, ROWS), ROWS)
-    source[own, :] = lax.dot_general(
-        fx[...], wcol[...], (((0,), (0,)), ((), ())), preferred_element_type=F32
-    ).astype(BF16)
-
-    def wait_chunk(chunk, carry):
+    source_copy.wait()
+
+    def step(chunk, carry):
         tile_copy(chunk).wait()
-        return carry
-
-    lax.fori_loop(0, (live + CHUNK - 1) // CHUNK, wait_chunk, 0)
-
-    def step(index, carry):
-        for k in range(F_UNROLL):
-            t = index * F_UNROLL + k
+        for k in range(CHUNK):
+            t = chunk * CHUNK + k
             rows = pl.ds(pl.multiple_of(src_ref[t] * TILE, TILE), TILE)
             product = dot(tiles[t], source[rows, :])
             d = jnp.where(t < live, dst_ref[t], PER)
             acc[pl.ds(d, 1)] = acc[pl.ds(d, 1)] + product[None]
         return carry
 
-    lax.fori_loop(0, (live + F_UNROLL - 1) // F_UNROLL, step, 0)
-
+    lax.fori_loop(0, chunks, step, 0)
+    for copy in late:
+        copy.wait()
     for d in range(PER):
         pre = acc[d]
         rows = pl.ds(d * TILE, TILE)
@@ -724,62 +695,57 @@
     return pltpu.CompilerParams(vmem_limit_bytes=62 * MIB, **fields)
 
 
-def call_gather(features, weight, refresh):
+def call_gather(features, weight, refresh, stale):
     return pl.pallas_call(
         gather_kernel,
         out_shape=(
             shape((PARTS, REF, TILE), BF16),
             shape((TILE, ROWS), BF16),
-            shape((TILE, TILE), BF16),
+            shape((PARTS * ROWS, TILE), BF16),
         ),
-        in_specs=[ANY] * 3,
+        in_specs=[ANY] * 4,
         out_specs=(ANY, ANY, ANY),
         scratch_shapes=[
             scratch((PARTS, REF, TILE), BF16),
+            scratch((PARTS * ROWS, TILE), BF16),
             scratch((TILE, REF), BF16),
             scratch((TILE, ROWS), BF16),
             scratch((64, 2 * TILE), BF16),
             scratch((TILE, TILE), BF16),
             scratch((PARTS, REF), I32),
-            DMA((63,)),
+            DMA((10, PER + 1)),
             DMA((PARTS,)),
             DMA((3,)),
             DMA((3,)),
             DMA((3,)),
-            DMA((4,)),
+            DMA,
+            DMA((3,)),
+            DMA((PARTS,)),
         ],
         compiler_params=params(collective_id=0, has_side_effects=True),
         name="gather_refreshed",
-    )(features, weight, refresh)
-
-
-def call_forward(
-    src, dst, count, refresh, fx, wcol, mask, gh, arr, stale, tiles, name="forward_tiles"
-):
+    )(features, weight, refresh, stale)
+
+
+def call_forward(src, dst, count, mask, gh, source, tiles, name="forward_tiles"):
     return pl.pallas_call(
         forward_kernel,
         out_shape=(shape((ROWS, TILE), BF16), shape((PER, TILE, TILE), BF16)),
-        in_specs=[SMEM] * 3 + [ANY] * 8,
+        in_specs=[SMEM] * 3 + [ANY] * 4,
         out_specs=(VMEM, VMEM),
         scratch_shapes=[
             scratch((PARTS * ROWS, TILE), BF16),
             scratch((NT, TILE, TILE), BF16),
-            scratch((PARTS, REF, TILE), BF16),
-            scratch((2, GROUP * REF, TILE), BF16),
             scratch((PER + 1, TILE, TILE), F32),
-            scratch((PARTS, REF), I32),
-            scratch((TILE, ROWS), BF16),
-            scratch((TILE, TILE), BF16),
             scratch((PER, TILE), I32),
             scratch((ROWS, TILE), BF16),
-            DMA((PARTS,)),
-            DMA((PARTS // GROUP,)),
+            DMA,
             DMA((NT // CHUNK,)),
-            DMA((5,)),
+            DMA((2,)),
         ],
         compiler_params=params(),
         name=name,
-    )(src, dst, count, refresh, fx, wcol, mask, gh, arr, stale, tiles)
+    )(src, dst, count, mask, gh, source, tiles)
 
 
 def call_backward(src, dst, count, refresh, fx, delta, arr, tiles, name="backward_tiles"):
@@ -855,20 +821,10 @@
     train_mask,
     grad_hidden,
 ):
-    arr, fx, wcol = call_gather(features.T, weight, refresh)
+    arr, fx, source = call_gather(features.T, weight, refresh, stale_cache)
     mask = train_mask.reshape(PER, TILE)
     hidden, delta = call_forward(
-        tile_src,
-        tile_dst,
-        tile_count,
-        refresh,
-        fx,
-        wcol,
-        mask,
-        grad_hidden,
-        arr,
-        stale_cache,
-        adj_tiles,
+        tile_src, tile_dst, tile_count, mask, grad_hidden, source, adj_tiles
     )
     picked, own, gw = call_backward(
         tile_src, tile_dst, tile_count, refresh, fx, delta, arr, adj_tiles

time: 142 us -> 142 us (level)
    pallas_call x1, Pallas kernels: 32 us -> 51.9 us  [call_gather(): pl.pallas_call(gather_kernel, out_shape=(shape((PARTS, REF, TILE), BF16),...]
    pallas_call x1, Pallas kernels: 47.3 us -> 33.8 us  [call_scatter(): pl.pallas_call(scatter_kernel, out_shape=(shape((64, ROWS), BF16), shape(...]
    pallas_call x1, Pallas kernels: 29.1 us -> 18.1 us  [call_forward(): pl.pallas_call(forward_kernel, out_shape=(shape((ROWS, TILE), BF16), shap...]
    pallas_call x1, Pallas kernels: 27.7 us -> 32.7 us  [call_backward(): pl.pallas_call(backward_kernel, out_shape=(shape((PARTS, TILE, REF), BF16...]
where the time goes in v3:
time: 142 us; the launch traced here: 141 us
  Pallas kernels  136 us (96%)
  local copies, waits for them, and re-layouts  3.04 us (2%)
    pallas_call x1, Pallas kernels, call_gather(): pl.pallas_call(gather_kernel, out_shape=(shape((PARTS, REF, TILE), BF16),...  51.9 us
    pallas_call x1, Pallas kernels, call_scatter(): pl.pallas_call(scatter_kernel, out_shape=(shape((64, ROWS), BF16), shape(...  33.8 us
    pallas_call x1, Pallas kernels, call_backward(): pl.pallas_call(backward_kernel, out_shape=(shape((PARTS, TILE, REF), BF16...  32.7 us
    pallas_call x1, Pallas kernels, call_forward(): pl.pallas_call(forward_kernel, out_shape=(shape((ROWS, TILE), BF16), shap...  18.1 us
    unnamed x2, local copies, waits for them, and re-layouts  3.04 us

profile of v3, /device:TPU:0, one launch (start us, length us, event | category | flops | bytes accessed | tf_op | source)
XLA Modules:
  0.0 140.8 jit_solution(8663104037375565997)
XLA Ops:
  1.3 51.9 %gather_refreshed.1 = (bf16[64,256,128]{2,1,0:T(8,128)(2,1)}, bf16[128,1024]{1,0:T(8,128)(2,1)}, bf16[65536,128]{1,0:T(8,128)(2,1)}) custom-call(bf16[64,1024]{1,0:T(8,128)(2,1)} %bitcast.3, bf16[64,256]{1,0:T(8,128)(2,1)} %w_hbm.3, s32[64,256]{1,0:T(8,128)} %refresh_hbm.5, bf16[65536,128]{1,0:T(8,128)(2,1)} %stale_hbm.1), custom_call_target="tpu_custom_call" | custom-call | tf_op jit(solution)/shard_map/gather_refreshed/pallas_call | solution.py:699
  53.2 18.1 %forward_tiles.1 = (bf16[1024,128]{1,0:T(8,128)(2,1)}, bf16[8,128,128]{2,1,0:T(8,128)(2,1)}) custom-call(s32[768]{0:T(1024)} %src_ref.3, s32[768]{0:T(1024)} %dst_ref.3, s32[1]{0:T(128)S(6)} %copy.15.count_ref, s32[8,128]{1,0:T(8,128)} %bitcast.5, bf16[1024,128]{1,0:T(8,128)(2,1)} %gh_hbm.1, bf16[65536,128]{1,0:T(8,128)(2,1)} %get-tuple-element.13.source_hbm, ...), custom_call_target="tpu_custom_call" | custom-call | tf_op jit(solution)/shard_map/forward_tiles/pallas_call | solution.py:731
  71.3 32.7 %backward_tiles.1 = (bf16[64,128,256]{2,1,0:T(8,128)(2,1)}, f32[128,1024]{1,0:T(8,128)}, f32[128,128]{1,0:T(8,128)}) custom-call(s32[768]{0:T(1024)} %src_ref.3, s32[768]{0:T(1024)} %dst_ref.3, s32[1]{0:T(128)S(6)} %copy.15.count_ref, s32[64,256]{1,0:T(8,128)} %refresh_hbm.5, bf16[128,1024]{1,0:T(8,128)(2,1)} %get-tuple-element.15.fx_hbm, ...), custom_call_target="tpu_custom_call" | custom-call | tf_op jit(solution)/shard_map/backward_tiles/pallas_call | solution.py:752
  104.0 33.8 %scatter_gradients.1 = (bf16[64,1024]{1,0:T(8,128)(2,1)}, f32[64,256]{1,0:T(8,128)}) custom-call(s32[64,256]{1,0:T(8,128)} %refresh_hbm.5, bf16[64,256]{1,0:T(8,128)(2,1)} %w_hbm.3, f32[128,1024]{1,0:T(8,128)} %get-tuple-element.18.own_hbm, f32[128,128]{1,0:T(8,128)} %get-tuple-element.19.gw_hbm, bf16[64,128,256]{2,1,0:T(8,128)(2,1)} %get-tuple-element.20.picked_hbm), custom_call_target="tpu_custom_call" | custom-call | tf_op jit(solution)/shard_map/scatter_gradients/pallas_call | solution.py:781
  137.8 1.6 %copy.16 = bf16[1024,64]{0,1:T(8,128)(2,1)} copy(bf16[1024,64]{0,1:T(8,128)(2,1)} %bitcast.4) | data formatting | bytes 262144
  139.3 1.5 %copy.17 = f32[64,256]{1,0:T(8,128)} copy(f32[64,256]{1,0:T(8,128)} %get-tuple-element.28) | data formatting | bytes 131072

commit v4 on v3

v4 whole, which is shorter than its diff:
```python
import jax
import jax.numpy as jnp
from jax import lax
from jax.experimental import pallas as pl
from jax.experimental.pallas import tpu as pltpu
from jax.sharding import PartitionSpec as P

MESH = pl.DeviceIdType.MESH
BF16 = jnp.bfloat16
F32 = jnp.float32
I32 = jnp.int32

ROWS = 1024
REF = 256
TILE = 128
NT = 768
PARTS = 64
BLOCKS = PARTS * ROWS // TILE
PER = ROWS // TILE
RING = 4
CLASS = PARTS // 2
MIB = 1024 * 1024


def dot(lhs, rhs):
    return jnp.dot(lhs, rhs, preferred_element_type=F32)


class Place:
    def __init__(self):
        self.dom = lax.axis_index("dom")
        self.feat = lax.axis_index("feat")
        self.core = self.dom % 2
        self.z = (self.dom // 2) % 2
        self.y = (self.dom // 4) % RING
        self.x = self.dom // 16
        self.a = self.x * (1 - self.core) + self.y * self.core
        self.b = self.y * (1 - self.core) + self.x * self.core
        self.sibling = self.dom + 1 - 2 * self.core
        self.z_pair = self.dom + 2 - 4 * self.z
        self.a_next = self.at(self.a + 1, self.b)
        self.a_prev = self.at(self.a + 3, self.b)
        self.b_next = self.at(self.a, self.b + 1)
        self.b_prev = self.at(self.a, self.b + 3)
        self.a_far = self.at(self.a + 2, self.b)
        self.b_far = self.at(self.a, self.b + 2)

    def at(self, a, b):
        a, b = a % RING, b % RING
        x = a * (1 - self.core) + b * self.core
        y = b * (1 - self.core) + a * self.core
        return ((x * RING + y) * 2 + self.z) * 2 + self.core

    def xy(self, x, y):
        return (((x % RING) * RING + y % RING) * 2 + self.z) * 2 + self.core

    def slot(self, a, b, z):
        return self.core * CLASS + (a % RING) * 8 + (b % RING) * 2 + z

    def greet(self, *more, cross=False):
        barrier = pltpu.get_barrier_semaphore()
        near = (self.sibling, self.z_pair, self.a_next, self.a_prev, self.b_next, self.b_prev)
        near = near + more
        for device in near:
            pl.semaphore_signal(barrier, inc=1, device_id=(device, self.feat), device_id_type=MESH)
        pairs = (self.dom, self.z_pair) if cross else (self.dom,)
        for device in pairs:
            pl.semaphore_signal(
                barrier, inc=1, device_id=(device, 1 - self.feat), device_id_type=MESH
            )
        return lambda: pl.semaphore_wait(barrier, len(near) + len(pairs))


def slot_part(slot):
    core, a, b, z = slot // CLASS, (slot // 8) % RING, (slot // 2) % RING, slot % 2
    x = a * (1 - core) + b * core
    y = b * (1 - core) + a * core
    return ((x * RING + y) * 2 + z) * 2 + core


def rows_by_refresh(row):
    column = jnp.transpose(jnp.broadcast_to(row, (TILE, REF)))
    lanes = lax.broadcasted_iota(I32, (REF, TILE), 1)
    parts = [(column == lanes + k * TILE).astype(F32).astype(BF16) for k in range(PER)]
    return jnp.concatenate(parts, axis=1)


def refresh_by_rows(row):
    rows = lax.broadcasted_iota(I32, (ROWS, REF), 0)
    return (rows == row).astype(F32).astype(BF16)


def fetch(sems, *pairs):
    copies = [pltpu.make_async_copy(src, dst, sems.at[k]) for k, (src, dst) in enumerate(pairs)]
    for copy in copies:
        copy.start()
    return copies


def half_rows(index):
    return pl.ds(pl.multiple_of(index * 64, 64), 64)


def column_block(index):
    return pl.ds(pl.multiple_of(index * TILE, TILE), TILE)


def plane(p):
    h = p // 2
    return (1 - h // 2) * 3 * h + (h // 2) * (h - 1), p % 2


def gather_kernel(
    feat_hbm,
    w_hbm,
    refresh_hbm,
    stale_hbm,
    arr_out,
    fx_out,
    source_out,
    arr,
    source,
    fresh_own,
    pick,
    fx,
    weight,
    wcol,
    refresh,
    send_sem,
    recv_sem,
    pair_send,
    pair_recv,
    give_sem,
    take_sem,
    load_sem,
    stale_sem,
    out_sem,
    row_sem,
):
    me = Place()
    f = me.feat
    own_rows, pair_rows = half_rows(f), half_rows(1 - f)
    own_columns, pair_columns = column_block(f), column_block(1 - f)
    loads = fetch(
        load_sem, (feat_hbm, fx.at[own_rows, :]), (w_hbm, weight), (refresh_hbm, refresh)
    )
    ready = me.greet(me.a_far)
    loads[2].wait()
    chosen = refresh_by_rows(refresh[pl.ds(me.dom, 1), :])
    loads[0].wait()
    pick[own_rows, :] = dot(fx[own_rows, :], chosen).astype(BF16)
    loads[1].wait()
    wcol[own_rows, :] = weight[:, own_columns]
    ready()

    def to_pair(k, src, dst):
        return pltpu.make_async_remote_copy(
            src_ref=src,
            dst_ref=dst,
            send_sem=pair_send.at[k],
            recv_sem=pair_recv.at[k],
            device_id=(me.dom, 1 - f),
            device_id_type=MESH,
        )

    pick_copy = to_pair(0, pick.at[own_rows, :], pick.at[own_rows, :])
    pick_copy.start()
    w_copy = to_pair(1, weight.at[:, pair_columns], wcol.at[own_rows, :])
    w_copy.start()
    fx_copy = to_pair(2, fx.at[own_rows, :], fx.at[own_rows, :])
    fx_copy.start()

    def shard(slot, target, kind, p):
        return pltpu.make_async_remote_copy(
            src_ref=arr.at[slot],
            dst_ref=arr.at[slot],
            send_sem=send_sem.at[kind, p],
            recv_sem=recv_sem.at[slot],
            device_id=(target, f),
            device_id_type=MESH,
        )

    def arrive(slot):
        shard(slot, me.sibling, 0, 0).wait_recv()

    def slot_of(p, b_offset):
        a_offset, pair = plane(p)
        return me.slot(me.a + a_offset, me.b + b_offset, (me.z + pair) % 2)

    def pass_on(p):
        slot = slot_of(p, 0)
        shard(slot, me.b_next, 0, p).start()
        shard(slot, me.b_prev, 1, p).start()

    def along_a(p):
        slot = slot_of(p, 0)
        shard(slot, me.a_next, 3, p).start()
        shard(slot, me.a_prev, 4, p).start()
        shard(slot, me.a_far, 5, p).start()

    def take_plane(p):
        slot = slot_of(p, 0)
        arrive(slot)
        return slot

    def take_b(p):
        below, above = slot_of(p, 3), slot_of(p, 1)
        arrive(below)

        @pl.when(p % 2 == 0)
        def _():
            shard(below, me.b_next, 2, p).start()

        arrive(above)

        @pl.when(p % 2 == 1)
        def _():
            shard(above, me.b_prev, 2, p).start()

        return below, above

    def take_far(p):
        slot = slot_of(p, 2)
        arrive(slot)
        return slot

    ones = jnp.ones((REF, TILE), BF16)

    class_first = me.core * CLASS

    def held(slot):
        return pl.ds(pl.multiple_of((slot - class_first) * ROWS, ROWS), ROWS)

    def rows_of(part):
        return pl.ds(pl.multiple_of(part * ROWS, ROWS), ROWS)

    def load_rows(slot):
        return pltpu.make_async_copy(
            stale_hbm.at[rows_of(slot_part(slot))], source.at[held(slot)], stale_sem.at[slot]
        )

    def keep_rows(slot):
        return pltpu.make_async_copy(
            source.at[held(slot)], source_out.at[rows_of(slot_part(slot))], row_sem.at[slot]
        )

    def give_rows(slot, src):
        return pltpu.make_async_remote_copy(
            src_ref=src,
            dst_ref=source_out.at[rows_of(slot_part(slot))],
            send_sem=give_sem.at[slot],
            recv_sem=take_sem.at[slot],
            device_id=(me.sibling, f),
            device_id_type=MESH,
        )

    def merge(*slots):
        fresh = [dot(arr[pl.ds(slot, 1)][0], wcol[...]).astype(BF16) for slot in slots]
        for slot, new in zip(slots, fresh):
            chosen = refresh_by_rows(refresh[pl.ds(slot_part(slot), 1), :])
            placed = dot(chosen, jnp.concatenate([new, ones], axis=1))
            rows = held(slot)
            old = source[rows, :].astype(F32)
            source[rows, :] = jnp.where(placed[:, TILE:] > 0, placed[:, :TILE], old).astype(BF16)
        for slot in slots:
            give_rows(slot, source.at[held(slot)]).start()

    def keep(*slots):
        for slot in slots:
            keep_rows(slot).start()

    mine = slot_of(0, 0)
    pick_copy.wait_recv()
    arr[pl.ds(mine, 1)] = jnp.transpose(pick[...].astype(F32)).astype(BF16)[None]
    pair_sent = shard(mine, me.z_pair, 2, PER)
    pair_sent.start()
    along_a(0)
    pass_on(0)

    def start_load(k, carry):
        load_rows(class_first + k).start()
        return carry

    def wait_load(k, carry):
        load_rows(class_first + k).wait()
        return carry

    lax.fori_loop(0, CLASS, start_load, 0)
    first = take_plane(1)
    along_a(1)
    pass_on(1)
    below, above = take_b(0)
    w_copy.wait_recv()
    lax.fori_loop(0, CLASS, wait_load, 0)
    merge(first, below, above, mine)
    keep(first, below, above)

    def relay(i, carry):
        near = take_plane(i + 1)
        pass_on(i + 1)
        below, above = take_b(i)
        far = take_far(i - 1)
        merge(near, below, above, far)
        keep(near, below, above, far)
        return carry

    lax.fori_loop(1, PER - 1, relay, 0)
    below, above = take_b(PER - 1)
    far = take_far(PER - 2)
    last = take_far(PER - 1)
    keep_arr = pltpu.make_async_copy(arr.at[pl.ds(class_first, CLASS)], arr_out, out_sem.at[0])
    keep_arr.start()
    merge(below, above, far, last)
    keep(below, above, far, last)
    fx_copy.wait_recv()
    keep_fx = pltpu.make_async_copy(fx, fx_out, out_sem.at[1])
    keep_fx.start()
    fresh_own[...] = lax.dot_general(
        fx[...], wcol[...], (((0,), (0,)), ((), ())), preferred_element_type=F32
    ).astype(BF16)
    keep_own = pltpu.make_async_copy(fresh_own, source_out.at[rows_of(me.dom)], row_sem.at[mine])
    keep_own.start()

    def settle(p, carry):
        for kind in range(3):
            shard(mine, me.sibling, kind, p).wait_send()
        return carry

    lax.fori_loop(0, PER, settle, 0)
    for p in range(2):
        for kind in range(3, 6):
            shard(mine, me.sibling, kind, p).wait_send()
    pair_sent.wait_send()
    pick_copy.wait_send()
    w_copy.wait_send()
    fx_copy.wait_send()

    def settle_rows(k, carry):
        given, taken = class_first + k, CLASS - class_first + k
        give_rows(given, source.at[held(given)]).wait_send()
        give_rows(taken, source_out.at[rows_of(slot_part(taken))]).wait_recv()
        keep_rows(class_first + k).wait()
        return carry

    lax.fori_loop(0, CLASS, settle_rows, 0)
    keep_fx.wait()
    keep_arr.wait()


GROUP = 8
CHUNK = 64


def forward_kernel(
    src_ref,
    dst_ref,
    count_ref,
    mask_hbm,
    gh_hbm,
    source_hbm,
    tiles_hbm,
    hidden_ref,
    delta_ref,
    source,
    tiles,
    acc,
    mask,
    gh,
    source_sem,
    tile_sem,
    load_sem,
):
    live = count_ref[0]
    chunks = (live + CHUNK - 1) // CHUNK
    source_copy = pltpu.make_async_copy(source_hbm, source, source_sem)
    source_copy.start()

    def tile_copy(chunk):
        part = pl.ds(chunk * CHUNK, CHUNK)
        return pltpu.make_async_copy(tiles_hbm.at[part], tiles.at[part], tile_sem.at[chunk])

    def start_chunk(chunk, carry):
        tile_copy(chunk).start()
        return carry

    lax.fori_loop(0, chunks, start_chunk, 0)
    late = fetch(load_sem, (mask_hbm, mask), (gh_hbm, gh))
    acc[...] = jnp.zeros_like(acc)
    source_copy.wait()

    def step(chunk, carry):
        tile_copy(chunk).wait()
        for k in range(CHUNK):
            t = chunk * CHUNK + k
            rows = pl.ds(pl.multiple_of(src_ref[t] * TILE, TILE), TILE)
            product = dot(tiles[t], source[rows, :])
            d = jnp.where(t < live, dst_ref[t], PER)
            acc[pl.ds(d, 1)] = acc[pl.ds(d, 1)] + product[None]
        return carry

    lax.fori_loop(0, chunks, step, 0)
    for copy in late:
        copy.wait()
    for d in range(PER):
        pre = acc[d]
        rows = pl.ds(d * TILE, TILE)
        hidden_ref[rows, :] = jnp.maximum(pre, 0.0).astype(BF16)
        passed = jnp.where(pre > 0, gh[rows, :].astype(F32), 0.0)
        kept = mask[pl.ds(d, 1), :].astype(F32)
        delta_ref[d] = (jnp.transpose(passed) * kept).astype(BF16)


B_CHUNK = 64
B_RING = 4
B_UNROLL = 64


def backward_kernel(
    src_ref,
    dst_ref,
    count_ref,
    refresh_hbm,
    fx_hbm,
    delta_hbm,
    tiles_hbm,
    picked_hbm,
    own_ref,
    gw_ref,
    acc,
    refresh,
    fx,
    delta,
    tiles,
    picked,
    tile_sem,
    load_sem,
    out_sem,
):
    me = lax.axis_index("dom")
    live = count_ref[0]
    chunks = (live + B_CHUNK - 1) // B_CHUNK

    def tile_copy(chunk):
        part = pl.ds(chunk * B_CHUNK, B_CHUNK)
        place = chunk % B_RING
        return pltpu.make_async_copy(tiles_hbm.at[part], tiles.at[place], tile_sem.at[place])

    for k in range(B_RING - 1):

        @pl.when(k < chunks)
        def _():
            tile_copy(k).start()

    loads = fetch(load_sem, (delta_hbm, delta), (refresh_hbm, refresh), (fx_hbm, fx))

    def clear(index, carry):
        acc[pl.ds(index * PER, PER)] = jnp.zeros((PER, TILE, TILE), F32)
        return carry

    lax.fori_loop(0, BLOCKS // PER, clear, 0)
    acc[BLOCKS] = jnp.zeros((TILE, TILE), F32)
    for copy in loads:
        copy.wait()

    def take_chunk(chunk, carry):
        @pl.when(chunk + B_RING - 1 < chunks)
        def _():
            tile_copy(chunk + B_RING - 1).start()

        tile_copy(chunk).wait()
        place = chunk % B_RING

        def step(index, carry):
            for k in range(B_UNROLL):
                local = index * B_UNROLL + k
                t = chunk * B_CHUNK + local
                product = dot(delta[dst_ref[t]], tiles[place, local])
                s = jnp.where(t < live, src_ref[t], BLOCKS)
                acc[pl.ds(s, 1)] = acc[pl.ds(s, 1)] + product[None]
            return carry

        return lax.fori_loop(0, B_CHUNK // B_UNROLL, step, carry)

    lax.fori_loop(0, chunks, take_chunk, 0)

    def out_copy(slot):
        return pltpu.make_async_copy(picked.at[slot], picked_hbm.at[slot], out_sem.at[slot])

    def pick(group, carry):
        for k in range(GROUP):
            slot = group * GROUP + k
            part = slot_part(slot)
            chosen = refresh_by_rows(refresh[pl.ds(part, 1), :])
            blocks = [acc[part * PER + i].astype(BF16) for i in range(PER)]
            grads = dot(jnp.concatenate(blocks, axis=1), chosen)
            grads = jnp.where(part == me, 0.0, grads).astype(BF16)
            picked[pl.ds(slot, 1)] = grads[None]
            out_copy(slot).start()
        return carry

    lax.fori_loop(0, PARTS // GROUP, pick, 0)
    for k in range(PER):
        own_ref[:, pl.ds(k * TILE, TILE)] = acc[me * PER + k].astype(BF16)
    gw_ref[...] = lax.dot_general(
        own_ref[...], fx[...], (((1,), (1,)), ((), ())), preferred_element_type=F32
    )

    def wait_out(slot, carry):
        out_copy(slot).wait()
        return carry

    lax.fori_loop(0, PARTS, wait_out, 0)


def scatter_kernel(
    refresh_hbm,
    w_hbm,
    own_hbm,
    gw_hbm,
    arr_hbm,
    picked_hbm,
    gf_out,
    gw_out,
    refresh,
    weight,
    own,
    own_in,
    base,
    gw,
    arr,
    work,
    sib,
    from_b1,
    from_b2,
    from_a,
    from_z,
    sum_core,
    sum_y,
    sum_x,
    sum_last,
    load_sem,
    small_sem,
    send_sem,
    recv_sem,
):
    me = Place()
    ready = me.greet(me.a_far, me.b_far, cross=True)
    f, a, b, z = me.feat, me.a, me.b, me.z
    order = (2, 1, 3, 0)

    def first_of(center, h):
        return ((center + order[h]) % RING) * 8

    loads = []
    for h in range(RING):
        first = first_of(a, h)
        copy = pltpu.make_async_copy(
            picked_hbm.at[pl.ds(me.core * CLASS + first, 8)],
            work.at[pl.ds(first, 8)],
            load_sem.at[h],
        )
        copy.start()
        loads.append(copy)
    small = fetch(
        small_sem,
        (arr_hbm, arr),
        (gw_hbm, gw),
        (own_hbm, own),
        (w_hbm, weight),
        (refresh_hbm, refresh),
    )
    ready()
    sends = []

    def send(src, dst, target, feat=None):
        k = len(sends)
        copy = pltpu.make_async_remote_copy(
            src_ref=src,
            dst_ref=dst,
            send_sem=send_sem.at[k],
            recv_sem=recv_sem.at[k],
            device_id=(target, f if feat is None else feat),
            device_id_type=MESH,
        )
        copy.start()
        sends.append(copy)
        return copy

    def add(first, size, *others):
        part = pl.ds(first, size)
        total = work[part].astype(F32)
        for other in others:
            total = total + other.astype(F32)
        work[part] = total.astype(BF16)

    to_sib = []
    for h in range(RING):
        first = first_of(b, h)
        src = picked_hbm.at[pl.ds((1 - me.core) * CLASS + first, 8)]
        to_sib.append(send(src, sib.at[pl.ds(first, 8)], me.sibling))
    own_copy = send(own_hbm, own_in, me.dom, 1 - f)

    def column(h, offset):
        return first_of(a, h) + ((b + offset) % RING) * 2

    b1, b2 = [], []

    def fold(h):
        first = first_of(a, h)
        loads[h].wait()
        to_sib[h].wait_recv()
        add(first, 8, sib[pl.ds(first, 8)])
        far, up, down = column(h, 2), column(h, 1), column(h, 3)
        b1.append(
            (
                send(work.at[pl.ds(far, 1)], from_b1.at[h, pl.ds(0, 1)], me.b_next),
                send(work.at[pl.ds(far + 1, 1)], from_b1.at[h, pl.ds(1, 1)], me.b_prev),
            )
        )
        b2.append(
            [
                send(work.at[pl.ds(up + 1, 1)], from_b2.at[h, 0, pl.ds(1, 1)], me.b_next),
                send(work.at[pl.ds(down, 1)], from_b2.at[h, 1, pl.ds(0, 1)], me.b_prev),
            ]
        )

    def weigh(h):
        first = first_of(a, h)
        total = gw[...]
        for k in range(8):
            total = total + dot(work[pl.ds(first + k, 1)][0], arr[pl.ds(first + k, 1)][0])
        gw[...] = total

    def relay(h):
        up, down = column(h, 1), column(h, 3)
        b1[h][0].wait_recv()
        add(up, 1, from_b1[h, pl.ds(0, 1)])
        b2[h].append(send(work.at[pl.ds(up, 1)], from_b2.at[h, 0, pl.ds(0, 1)], me.b_next))
        b1[h][1].wait_recv()
        add(down + 1, 1, from_b1[h, pl.ds(1, 1)])
        b2[h].append(send(work.at[pl.ds(down + 1, 1)], from_b2.at[h, 1, pl.ds(1, 1)], me.b_prev))

    along_a = []
    a_targets = (me.a_far, me.a_next, me.a_prev)

    def finish(h):
        here = column(h, 0)
        for copy in b2[h]:
            copy.wait_recv()
        if h < 3:
            add(here, 2, from_b2[h, 0], from_b2[h, 1])
            along_a.append(send(work.at[pl.ds(here, 2)], from_a.at[h], a_targets[h]))
        else:
            for copy in along_a:
                copy.wait_recv()
            add(here, 2, from_b2[h, 0], from_b2[h, 1], from_a[0], from_a[1], from_a[2])

    def ring_sum(buffer, index, targets):
        return [send(buffer.at[index], buffer.at[index], target) for target in targets]

    def take_sum(buffer, copies):
        for copy in copies:
            copy.wait_recv()
        return (buffer[0] + buffer[1]) + (buffer[2] + buffer[3])

    fold(0)
    small[0].wait()
    small[1].wait()
    fold(1)
    weigh(0)
    relay(0)
    fold(2)
    weigh(1)
    relay(1)
    fold(3)
    weigh(2)
    finish(0)
    weigh(3)
    sum_core[0] = jnp.transpose(gw[...])
    core_copy = send(sum_core.at[0], sum_core.at[1], me.sibling)
    relay(2)
    finish(1)
    relay(3)
    core_copy.wait_recv()
    sum_y[pl.ds(me.y, 1)] = (sum_core[0] + sum_core[1])[None]
    y_targets = [me.xy(me.x, me.y + k) for k in (1, 3, 2)]
    y_copies = ring_sum(sum_y, me.y, y_targets)
    finish(2)
    for copy in small[2:]:
        copy.wait()
    chosen = rows_by_refresh(refresh[pl.ds(me.dom, 1), :])
    own_columns, other_columns = column_block(f), column_block(1 - f)
    own_copy.wait_recv()
    base[...] = dot(weight[:, own_columns], own[...]) + dot(weight[:, other_columns], own_in[...])
    sum_x[pl.ds(me.x, 1)] = take_sum(sum_y, y_copies)[None]
    x_targets = [me.xy(me.x + k, me.y) for k in (1, 3, 2)]
    x_copies = ring_sum(sum_x, me.x, x_targets)
    finish(3)
    here = column(3, 0)
    mine, theirs = work.at[pl.ds(here + z, 1)], work.at[pl.ds(here + 1 - z, 1)]
    z_copies = (
        send(theirs, from_z.at[pl.ds(0, 1)], me.z_pair),
        send(mine, from_z.at[pl.ds(1, 1)], me.dom, 1 - f),
        send(theirs, from_z.at[pl.ds(2, 1)], me.z_pair, 1 - f),
    )
    sum_last[0] = take_sum(sum_x, x_copies)
    own_rows, other_rows = half_rows(f), half_rows(1 - f)
    last_copies = (
        send(sum_last.at[0, own_rows, :], sum_last.at[1, pl.ds(0, 64), :], me.z_pair),
        send(sum_last.at[0, other_rows, :], sum_last.at[1, pl.ds(64, 64), :], me.dom, 1 - f),
        send(sum_last.at[0, other_rows, :], sum_last.at[2, pl.ds(0, 64), :], me.z_pair, 1 - f),
    )
    for copy in z_copies:
        copy.wait_recv()
    carried = work[pl.ds(here + z, 1)][0].astype(F32) + from_z[0].astype(F32)
    carried_in = from_z[1].astype(F32) + from_z[2].astype(F32)
    short = dot(weight[:, own_columns], carried.astype(BF16)) + dot(
        weight[:, other_columns], carried_in.astype(BF16)
    )
    gf_out[...] = (base[...] + dot(short.astype(BF16), chosen)).astype(BF16)
    for copy in last_copies:
        copy.wait_recv()
    gw_out[:, own_columns] = sum_last[0, own_rows, :] + sum_last[1, pl.ds(0, 64), :]
    gw_out[:, other_columns] = sum_last[1, pl.ds(64, 64), :] + sum_last[2, pl.ds(0, 64), :]
    for copy in sends:
        copy.wait_send()


VMEM = pl.BlockSpec(memory_space=pltpu.VMEM)
SMEM = pl.BlockSpec(memory_space=pltpu.SMEM)
ANY = pl.BlockSpec(memory_space=pl.ANY)
DMA = pltpu.SemaphoreType.DMA


def shape(dims, kind):
    return jax.ShapeDtypeStruct(dims, kind)


def scratch(dims, kind):
    return pltpu.VMEM(dims, kind)


def params(**fields):
    return pltpu.CompilerParams(vmem_limit_bytes=62 * MIB, **fields)


def call_gather(features, weight, refresh, stale):
    return pl.pallas_call(
        gather_kernel,
        out_shape=(
            shape((CLASS, REF, TILE), BF16),
            shape((TILE, ROWS), BF16),
            shape((PARTS * ROWS, TILE), BF16),
        ),
        in_specs=[ANY] * 4,
        out_specs=(ANY, ANY, ANY),
        scratch_shapes=[
            scratch((PARTS, REF, TILE), BF16),
            scratch((CLASS * ROWS, TILE), BF16),
            scratch((ROWS, TILE), BF16),
            scratch((TILE, REF), BF16),
            scratch((TILE, ROWS), BF16),
            scratch((64, 2 * TILE), BF16),
            scratch((TILE, TILE), BF16),
            scratch((PARTS, REF), I32),
            DMA((6, PER + 1)),
            DMA((PARTS,)),
            DMA((3,)),
            DMA((3,)),
            DMA((PARTS,)),
            DMA((PARTS,)),
            DMA((3,)),
            DMA((PARTS,)),
            DMA((2,)),
            DMA((PARTS,)),
        ],
        compiler_params=params(collective_id=0, has_side_effects=True),
        name="gather_refreshed",
    )(features, weight, refresh, stale)


def call_forward(src, dst, count, mask, gh, source, tiles, name="forward_tiles"):
    return pl.pallas_call(
        forward_kernel,
        out_shape=(shape((ROWS, TILE), BF16), shape((PER, TILE, TILE), BF16)),
        in_specs=[SMEM] * 3 + [ANY] * 4,
        out_specs=(VMEM, VMEM),
        scratch_shapes=[
            scratch((PARTS * ROWS, TILE), BF16),
            scratch((NT, TILE, TILE), BF16),
            scratch((PER + 1, TILE, TILE), F32),
            scratch((PER, TILE), I32),
            scratch((ROWS, TILE), BF16),
            DMA,
            DMA((NT // CHUNK,)),
            DMA((2,)),
        ],
        compiler_params=params(),
        name=name,
    )(src, dst, count, mask, gh, source, tiles)


def call_backward(src, dst, count, refresh, fx, delta, tiles, name="backward_tiles"):
    return pl.pallas_call(
        backward_kernel,
        out_shape=(
            shape((PARTS, TILE, REF), BF16),
            shape((TILE, ROWS), BF16),
            shape((TILE, TILE), F32),
        ),
        in_specs=[SMEM] * 3 + [ANY] * 4,
        out_specs=(ANY, VMEM, VMEM),
        scratch_shapes=[
            scratch((BLOCKS + 1, TILE, TILE), F32),
            scratch((PARTS, REF), I32),
            scratch((TILE, ROWS), BF16),
            scratch((PER, TILE, TILE), BF16),
            scratch((B_RING, B_CHUNK, TILE, TILE), BF16),
            scratch((PARTS, TILE, REF), BF16),
            DMA((B_RING,)),
            DMA((3,)),
            DMA((PARTS,)),
        ],
        compiler_params=params(),
        name=name,
    )(src, dst, count, refresh, fx, delta, tiles)


def call_scatter(refresh, weight, own, gw, arr, picked):
    return pl.pallas_call(
        scatter_kernel,
        out_shape=(shape((64, ROWS), BF16), shape((64, 2 * TILE), F32)),
        in_specs=[ANY] * 6,
        out_specs=(VMEM, VMEM),
        scratch_shapes=[
            scratch((PARTS, REF), I32),
            scratch((64, 2 * TILE), BF16),
            scratch((TILE, ROWS), BF16),
            scratch((TILE, ROWS), BF16),
            scratch((64, ROWS), F32),
            scratch((TILE, TILE), F32),
            scratch((CLASS, REF, TILE), BF16),
            scratch((CLASS, TILE, REF), BF16),
            scratch((CLASS, TILE, REF), BF16),
            scratch((RING, 2, TILE, REF), BF16),
            scratch((RING, 2, 2, TILE, REF), BF16),
            scratch((3, 2, TILE, REF), BF16),
            scratch((3, TILE, REF), BF16),
            scratch((2, TILE, TILE), F32),
            scratch((RING, TILE, TILE), F32),
            scratch((RING, TILE, TILE), F32),
            scratch((3, TILE, TILE), F32),
            DMA((RING,)),
            DMA((5,)),
            DMA((48,)),
            DMA((48,)),
        ],
        compiler_params=params(collective_id=1, has_side_effects=True),
        name="scatter_gradients",
    )(refresh, weight, own, gw, arr, picked)


def shards(
    features,
    weight,
    stale_cache,
    adj_tiles,
    tile_src,
    tile_dst,
    tile_count,
    refresh,
    train_mask,
    grad_hidden,
):
    arr, fx, source = call_gather(features.T, weight, refresh, stale_cache)
    mask = train_mask.reshape(PER, TILE)
    hidden, delta = call_forward(
        tile_src, tile_dst, tile_count, mask, grad_hidden, source, adj_tiles
    )
    picked, own, gw = call_backward(
        tile_src, tile_dst, tile_count, refresh, fx, delta, adj_tiles
    )
    grad_features, grad_weight = call_scatter(refresh, weight, own, gw, arr, picked)
    return hidden, grad_features.T, grad_weight


def solution(mesh):
    placed = (
        P("dom", "feat"),
        P("feat", None),
        P(None, "feat"),
        P("dom", None, None),
        P("dom"),
        P("dom"),
        P("dom"),
        P(),
        P("dom"),
        P("dom", "feat"),
    )
    return jax.shard_map(
        shards,
        mesh=mesh,
        in_specs=placed,
        out_specs=(P("dom", "feat"), P("dom", "feat"), P("feat", None)),
        check_vma=False,
    )
```

time: 142 us -> 123 us (0.87)
  Pallas kernels: 136 us -> 119 us
    pallas_call x1, Pallas kernels: 32.7 us -> 15 us  [call_backward(): pl.pallas_call(backward_kernel, out_shape=(shape((PARTS, TILE, REF), BF16...]
    pallas_call x1, Pallas kernels: 33.8 us -> 48.1 us  [call_scatter(): pl.pallas_call(scatter_kernel, out_shape=(shape((64, ROWS), BF16), shape(...]
    pallas_call x1, Pallas kernels: 18.1 us -> 10.6 us  [call_forward(): pl.pallas_call(forward_kernel, out_shape=(shape((ROWS, TILE), BF16), shap...]
    pallas_call x1, Pallas kernels: 51.9 us -> 44.9 us  [call_gather(): pl.pallas_call(gather_kernel, out_shape=(shape((CLASS, REF, TILE), BF16),...]
where the time goes in v4:
time: 123 us
  Pallas kernels  119 us (97%)
  local copies, waits for them, and re-layouts  3.04 us (2%)
  between operations  1.31 us (1%)
    pallas_call x1, Pallas kernels, call_scatter(): pl.pallas_call(scatter_kernel, out_shape=(shape((64, ROWS), BF16), shape(...  48.1 us
    pallas_call x1, Pallas kernels, call_gather(): pl.pallas_call(gather_kernel, out_shape=(shape((CLASS, REF, TILE), BF16),...  44.9 us
    pallas_call x1, Pallas kernels, call_backward(): pl.pallas_call(backward_kernel, out_shape=(shape((PARTS, TILE, REF), BF16...  15 us
    pallas_call x1, Pallas kernels, call_forward(): pl.pallas_call(forward_kernel, out_shape=(shape((ROWS, TILE), BF16), shap...  10.6 us
    unnamed x2, local copies, waits for them, and re-layouts  3.04 us

profile of v4, /device:TPU:0, one launch (start us, length us, event | category | flops | bytes accessed | tf_op | source)
XLA Modules:
  0.0 123.0 jit_solution(10047684149049135437)
XLA Ops:
  1.3 44.9 %gather_refreshed.1 = (bf16[32,256,128]{2,1,0:T(8,128)(2,1)}, bf16[128,1024]{1,0:T(8,128)(2,1)}, bf16[65536,128]{1,0:T(8,128)(2,1)}) custom-call(bf16[64,1024]{1,0:T(8,128)(2,1)} %bitcast.3, bf16[64,256]{1,0:T(8,128)(2,1)} %w_hbm.3, s32[64,256]{1,0:T(8,128)} %refresh_hbm.5, bf16[65536,128]{1,0:T(8,128)(2,1)} %stale_hbm.1), custom_call_target="tpu_custom_call" | custom-call | tf_op jit(solution)/shard_map/gather_refreshed/pallas_call | solution.py:748
  46.1 10.6 %forward_tiles.1 = (bf16[1024,128]{1,0:T(8,128)(2,1)}, bf16[8,128,128]{2,1,0:T(8,128)(2,1)}) custom-call(s32[768]{0:T(1024)} %src_ref.3, s32[768]{0:T(1024)} %dst_ref.3, s32[1]{0:T(128)S(6)} %copy.15.count_ref, s32[8,128]{1,0:T(8,128)} %bitcast.5, bf16[1024,128]{1,0:T(8,128)(2,1)} %gh_hbm.1, bf16[65536,128]{1,0:T(8,128)(2,1)} %get-tuple-element.13.source_hbm, ...), custom_call_target="tpu_custom_call" | custom-call | tf_op jit(solution)/shard_map/forward_tiles/pallas_call | solution.py:783
  56.8 15.0 %backward_tiles.1 = (bf16[64,128,256]{2,1,0:T(8,128)(2,1)}, bf16[128,1024]{1,0:T(8,128)(2,1)}, f32[128,128]{1,0:T(8,128)}) custom-call(s32[768]{0:T(1024)} %src_ref.3, s32[768]{0:T(1024)} %dst_ref.3, s32[1]{0:T(128)S(6)} %copy.15.count_ref, s32[64,256]{1,0:T(8,128)} %refresh_hbm.5, bf16[128,1024]{1,0:T(8,128)(2,1)} %get-tuple-element.15.fx_hbm, ...), custom_call_target="tpu_custom_call" | custom-call | tf_op jit(solution)/shard_map/backward_tiles/pallas_call | solution.py:804
  71.8 48.1 %scatter_gradients.1 = (bf16[64,1024]{1,0:T(8,128)(2,1)}, f32[64,256]{1,0:T(8,128)}) custom-call(s32[64,256]{1,0:T(8,128)} %refresh_hbm.5, bf16[64,256]{1,0:T(8,128)(2,1)} %w_hbm.3, bf16[128,1024]{1,0:T(8,128)(2,1)} %get-tuple-element.17.own_hbm, f32[128,128]{1,0:T(8,128)} %get-tuple-element.18.gw_hbm, bf16[32,256,128]{2,1,0:T(8,128)(2,1)} %get-tuple-element.19.arr_hbm, ...), custom_call_target="tpu_custom_call" | custom-call | tf_op jit(solution)/shard_map/scatter_gradients/pallas_call | solution.py:830
  119.9 1.6 %copy.16 = bf16[1024,64]{0,1:T(8,128)(2,1)} copy(bf16[1024,64]{0,1:T(8,128)(2,1)} %bitcast.4) | data formatting | bytes 262144
  121.5 1.5 %copy.17 = f32[64,256]{1,0:T(8,128)} copy(f32[64,256]{1,0:T(8,128)} %get-tuple-element.28) | data formatting | bytes 131072

commit v5 on v4

--- a/solution.py
+++ b/solution.py
@@ -105,9 +105,7 @@
     return pl.ds(pl.multiple_of(index * TILE, TILE), TILE)
 
 
-def plane(p):
-    h = p // 2
-    return (1 - h // 2) * 3 * h + (h // 2) * (h - 1), p % 2
+PLANE = ((0, 0), (0, 1), (3, 0), (1, 0), (3, 1), (1, 1), (2, 0), (2, 1))
 
 
 def gather_kernel(
@@ -184,7 +182,7 @@
         shard(slot, me.sibling, 0, 0).wait_recv()
 
     def slot_of(p, b_offset):
-        a_offset, pair = plane(p)
+        a_offset, pair = PLANE[p]
         return me.slot(me.a + a_offset, me.b + b_offset, (me.z + pair) % 2)
 
     def pass_on(p):
@@ -201,22 +199,19 @@
     def take_plane(p):
         slot = slot_of(p, 0)
         arrive(slot)
+        if p == 1:
+            along_a(p)
+        pass_on(p)
         return slot
 
     def take_b(p):
         below, above = slot_of(p, 3), slot_of(p, 1)
         arrive(below)
-
-        @pl.when(p % 2 == 0)
-        def _():
+        if PLANE[p][1] == 0:
             shard(below, me.b_next, 2, p).start()
-
         arrive(above)
-
-        @pl.when(p % 2 == 1)
-        def _():
+        if PLANE[p][1] == 1:
             shard(above, me.b_prev, 2, p).start()
-
         return below, above
 
     def take_far(p):
@@ -253,6 +248,8 @@
             device_id=(me.sibling, f),
             device_id_type=MESH,
         )
+
+    mine = slot_of(0, 0)
 
     def merge(*slots):
         fresh = [dot(arr[pl.ds(slot, 1)][0], wcol[...]).astype(BF16) for slot in slots]
@@ -264,12 +261,9 @@
             source[rows, :] = jnp.where(placed[:, TILE:] > 0, placed[:, :TILE], old).astype(BF16)
         for slot in slots:
             give_rows(slot, source.at[held(slot)]).start()
-
-    def keep(*slots):
-        for slot in slots:
-            keep_rows(slot).start()
-
-    mine = slot_of(0, 0)
+            if slot is not mine:
+                keep_rows(slot).start()
+
     pick_copy.wait_recv()
     arr[pl.ds(mine, 1)] = jnp.transpose(pick[...].astype(F32)).astype(BF16)[None]
     pair_sent = shard(mine, me.z_pair, 2, PER)
@@ -286,32 +280,30 @@
         return carry
 
     lax.fori_loop(0, CLASS, start_load, 0)
-    first = take_plane(1)
-    along_a(1)
-    pass_on(1)
-    below, above = take_b(0)
+    left, right = take_plane(2), take_plane(3)
+    b0 = take_b(0)
+    z_pair = take_plane(1)
+    across = take_plane(6)
     w_copy.wait_recv()
     lax.fori_loop(0, CLASS, wait_load, 0)
-    merge(first, below, above, mine)
-    keep(first, below, above)
-
-    def relay(i, carry):
-        near = take_plane(i + 1)
-        pass_on(i + 1)
-        below, above = take_b(i)
-        far = take_far(i - 1)
-        merge(near, below, above, far)
-        keep(near, below, above, far)
-        return carry
-
-    lax.fori_loop(1, PER - 1, relay, 0)
-    below, above = take_b(PER - 1)
-    far = take_far(PER - 2)
-    last = take_far(PER - 1)
+    merge(left, right, *b0)
+    merge(z_pair, across, mine)
+    left, right = take_plane(4), take_plane(5)
+    b2, b3 = take_b(2), take_b(3)
+    merge(left, right, *b2)
+    across = take_plane(7)
+    b1, b6 = take_b(1), take_b(6)
+    merge(*b3, *b1)
+    b4, b5 = take_b(4), take_b(5)
+    far0 = take_far(0)
+    merge(*b6, across, far0)
+    b7 = take_b(7)
+    merge(*b4, *b5)
+    merge(*b7, take_far(2), take_far(3))
+    merge(take_far(1), take_far(6), take_far(4), take_far(5))
+    merge(take_far(7))
     keep_arr = pltpu.make_async_copy(arr.at[pl.ds(class_first, CLASS)], arr_out, out_sem.at[0])
     keep_arr.start()
-    merge(below, above, far, last)
-    keep(below, above, far, last)
     fx_copy.wait_recv()
     keep_fx = pltpu.make_async_copy(fx, fx_out, out_sem.at[1])
     keep_fx.start()
@@ -349,109 +341,61 @@
 
 GROUP = 8
 CHUNK = 64
-
-
-def forward_kernel(
+TILE_RING = 3
+STAGED = 16
+
+
+def tiles_kernel(
     src_ref,
     dst_ref,
     count_ref,
+    refresh_hbm,
+    fx_hbm,
     mask_hbm,
     gh_hbm,
     source_hbm,
     tiles_hbm,
     hidden_ref,
-    delta_ref,
-    source,
-    tiles,
-    acc,
-    mask,
-    gh,
-    source_sem,
-    tile_sem,
-    load_sem,
-):
-    live = count_ref[0]
-    chunks = (live + CHUNK - 1) // CHUNK
-    source_copy = pltpu.make_async_copy(source_hbm, source, source_sem)
-    source_copy.start()
-
-    def tile_copy(chunk):
-        part = pl.ds(chunk * CHUNK, CHUNK)
-        return pltpu.make_async_copy(tiles_hbm.at[part], tiles.at[part], tile_sem.at[chunk])
-
-    def start_chunk(chunk, carry):
-        tile_copy(chunk).start()
-        return carry
-
-    lax.fori_loop(0, chunks, start_chunk, 0)
-    late = fetch(load_sem, (mask_hbm, mask), (gh_hbm, gh))
-    acc[...] = jnp.zeros_like(acc)
-    source_copy.wait()
-
-    def step(chunk, carry):
-        tile_copy(chunk).wait()
-        for k in range(CHUNK):
-            t = chunk * CHUNK + k
-            rows = pl.ds(pl.multiple_of(src_ref[t] * TILE, TILE), TILE)
-            product = dot(tiles[t], source[rows, :])
-            d = jnp.where(t < live, dst_ref[t], PER)
-            acc[pl.ds(d, 1)] = acc[pl.ds(d, 1)] + product[None]
-        return carry
-
-    lax.fori_loop(0, chunks, step, 0)
-    for copy in late:
-        copy.wait()
-    for d in range(PER):
-        pre = acc[d]
-        rows = pl.ds(d * TILE, TILE)
-        hidden_ref[rows, :] = jnp.maximum(pre, 0.0).astype(BF16)
-        passed = jnp.where(pre > 0, gh[rows, :].astype(F32), 0.0)
-        kept = mask[pl.ds(d, 1), :].astype(F32)
-        delta_ref[d] = (jnp.transpose(passed) * kept).astype(BF16)
-
-
-B_CHUNK = 64
-B_RING = 4
-B_UNROLL = 64
-
-
-def backward_kernel(
-    src_ref,
-    dst_ref,
-    count_ref,
-    refresh_hbm,
-    fx_hbm,
-    delta_hbm,
-    tiles_hbm,
     picked_hbm,
     own_ref,
     gw_ref,
+    source,
+    tiles,
+    pre,
     acc,
+    delta,
     refresh,
     fx,
-    delta,
-    tiles,
+    mask,
+    gh,
     picked,
+    source_sem,
     tile_sem,
     load_sem,
     out_sem,
 ):
     me = lax.axis_index("dom")
     live = count_ref[0]
-    chunks = (live + B_CHUNK - 1) // B_CHUNK
-
-    def tile_copy(chunk):
-        part = pl.ds(chunk * B_CHUNK, B_CHUNK)
-        place = chunk % B_RING
+    chunks = (live + CHUNK - 1) // CHUNK
+    source_copy = pltpu.make_async_copy(source_hbm, source, source_sem)
+    source_copy.start()
+
+    def tile_copy(turn):
+        chunk = jnp.where(turn < chunks, turn, turn - chunks)
+        place = turn % TILE_RING
+        part = pl.ds(chunk * CHUNK, CHUNK)
         return pltpu.make_async_copy(tiles_hbm.at[part], tiles.at[place], tile_sem.at[place])
 
-    for k in range(B_RING - 1):
-
-        @pl.when(k < chunks)
+    for turn in range(TILE_RING):
+
+        @pl.when(turn < 2 * chunks)
         def _():
-            tile_copy(k).start()
-
-    loads = fetch(load_sem, (delta_hbm, delta), (refresh_hbm, refresh), (fx_hbm, fx))
+            tile_copy(turn).start()
+
+    loads = fetch(
+        load_sem, (mask_hbm, mask), (gh_hbm, gh), (refresh_hbm, refresh), (fx_hbm, fx)
+    )
+    pre[...] = jnp.zeros_like(pre)
 
     def clear(index, carry):
         acc[pl.ds(index * PER, PER)] = jnp.zeros((PER, TILE, TILE), F32)
@@ -459,34 +403,62 @@
 
     lax.fori_loop(0, BLOCKS // PER, clear, 0)
     acc[BLOCKS] = jnp.zeros((TILE, TILE), F32)
+    source_copy.wait()
+
+    def next_tiles(turn):
+        @pl.when(turn + TILE_RING < 2 * chunks)
+        def _():
+            tile_copy(turn + TILE_RING).start()
+
+    def forward(chunk, carry):
+        tile_copy(chunk).wait()
+        place = chunk % TILE_RING
+        for k in range(CHUNK):
+            t = chunk * CHUNK + k
+            rows = pl.ds(pl.multiple_of(src_ref[t] * TILE, TILE), TILE)
+            product = dot(tiles[place, k], source[rows, :])
+            d = jnp.where(t < live, dst_ref[t], PER)
+            pre[pl.ds(d, 1)] = pre[pl.ds(d, 1)] + product[None]
+        next_tiles(chunk)
+        return carry
+
+    lax.fori_loop(0, chunks, forward, 0)
     for copy in loads:
         copy.wait()
-
-    def take_chunk(chunk, carry):
-        @pl.when(chunk + B_RING - 1 < chunks)
-        def _():
-            tile_copy(chunk + B_RING - 1).start()
-
-        tile_copy(chunk).wait()
-        place = chunk % B_RING
-
-        def step(index, carry):
-            for k in range(B_UNROLL):
-                local = index * B_UNROLL + k
-                t = chunk * B_CHUNK + local
-                product = dot(delta[dst_ref[t]], tiles[place, local])
-                s = jnp.where(t < live, src_ref[t], BLOCKS)
-                acc[pl.ds(s, 1)] = acc[pl.ds(s, 1)] + product[None]
-            return carry
-
-        return lax.fori_loop(0, B_CHUNK // B_UNROLL, step, carry)
-
-    lax.fori_loop(0, chunks, take_chunk, 0)
+    for d in range(PER):
+        total = pre[d]
+        rows = pl.ds(d * TILE, TILE)
+        hidden_ref[rows, :] = jnp.maximum(total, 0.0).astype(BF16)
+        passed = jnp.where(total > 0, gh[rows, :].astype(F32), 0.0)
+        kept = mask[pl.ds(d, 1), :].astype(F32)
+        delta[d] = (jnp.transpose(passed) * kept).astype(BF16)
+
+    def backward(chunk, carry):
+        turn = chunks + chunk
+        tile_copy(turn).wait()
+        place = turn % TILE_RING
+        for k in range(CHUNK):
+            t = chunk * CHUNK + k
+            product = dot(delta[dst_ref[t]], tiles[place, k])
+            s = jnp.where(t < live, src_ref[t], BLOCKS)
+            acc[pl.ds(s, 1)] = acc[pl.ds(s, 1)] + product[None]
+        next_tiles(turn)
+        return carry
+
+    lax.fori_loop(0, chunks, backward, 0)
 
     def out_copy(slot):
-        return pltpu.make_async_copy(picked.at[slot], picked_hbm.at[slot], out_sem.at[slot])
+        place = slot % STAGED
+        return pltpu.make_async_copy(picked.at[place], picked_hbm.at[slot], out_sem.at[place])
 
     def pick(group, carry):
+        for k in range(GROUP):
+            slot = group * GROUP + k
+
+            @pl.when(slot >= STAGED)
+            def _():
+                out_copy(slot - STAGED).wait()
+
         for k in range(GROUP):
             slot = group * GROUP + k
             part = slot_part(slot)
@@ -494,8 +466,9 @@
             blocks = [acc[part * PER + i].astype(BF16) for i in range(PER)]
             grads = dot(jnp.concatenate(blocks, axis=1), chosen)
             grads = jnp.where(part == me, 0.0, grads).astype(BF16)
-            picked[pl.ds(slot, 1)] = grads[None]
-            out_copy(slot).start()
+            picked[pl.ds(slot % STAGED, 1)] = grads[None]
+        for k in range(GROUP):
+            out_copy(group * GROUP + k).start()
         return carry
 
     lax.fori_loop(0, PARTS // GROUP, pick, 0)
@@ -504,12 +477,8 @@
     gw_ref[...] = lax.dot_general(
         own_ref[...], fx[...], (((1,), (1,)), ((), ())), preferred_element_type=F32
     )
-
-    def wait_out(slot, carry):
+    for slot in range(PARTS - STAGED, PARTS):
         out_copy(slot).wait()
-        return carry
-
-    lax.fori_loop(0, PARTS, wait_out, 0)
 
 
 def scatter_kernel(
@@ -779,51 +748,36 @@
     )(features, weight, refresh, stale)
 
 
-def call_forward(src, dst, count, mask, gh, source, tiles, name="forward_tiles"):
+def call_tiles(src, dst, count, refresh, fx, mask, gh, source, tiles, name="tiles"):
     return pl.pallas_call(
-        forward_kernel,
-        out_shape=(shape((ROWS, TILE), BF16), shape((PER, TILE, TILE), BF16)),
-        in_specs=[SMEM] * 3 + [ANY] * 4,
-        out_specs=(VMEM, VMEM),
-        scratch_shapes=[
-            scratch((PARTS * ROWS, TILE), BF16),
-            scratch((NT, TILE, TILE), BF16),
-            scratch((PER + 1, TILE, TILE), F32),
-            scratch((PER, TILE), I32),
-            scratch((ROWS, TILE), BF16),
-            DMA,
-            DMA((NT // CHUNK,)),
-            DMA((2,)),
-        ],
-        compiler_params=params(),
-        name=name,
-    )(src, dst, count, mask, gh, source, tiles)
-
-
-def call_backward(src, dst, count, refresh, fx, delta, tiles, name="backward_tiles"):
-    return pl.pallas_call(
-        backward_kernel,
+        tiles_kernel,
         out_shape=(
+            shape((ROWS, TILE), BF16),
             shape((PARTS, TILE, REF), BF16),
             shape((TILE, ROWS), BF16),
             shape((TILE, TILE), F32),
         ),
-        in_specs=[SMEM] * 3 + [ANY] * 4,
-        out_specs=(ANY, VMEM, VMEM),
+        in_specs=[SMEM] * 3 + [ANY] * 6,
+        out_specs=(VMEM, ANY, VMEM, VMEM),
         scratch_shapes=[
+            scratch((PARTS * ROWS, TILE), BF16),
+            scratch((TILE_RING, CHUNK, TILE, TILE), BF16),
+            scratch((PER + 1, TILE, TILE), F32),
             scratch((BLOCKS + 1, TILE, TILE), F32),
+            scratch((PER, TILE, TILE), BF16),
             scratch((PARTS, REF), I32),
             scratch((TILE, ROWS), BF16),
-            scratch((PER, TILE, TILE), BF16),
-            scratch((B_RING, B_CHUNK, TILE, TILE), BF16),
-            scratch((PARTS, TILE, REF), BF16),
-            DMA((B_RING,)),
-            DMA((3,)),
-            DMA((PARTS,)),
+            scratch((PER, TILE), I32),
+            scratch((ROWS, TILE), BF16),
+            scratch((STAGED, TILE, REF), BF16),
+            DMA,
+            DMA((TILE_RING,)),
+            DMA((4,)),
+            DMA((STAGED,)),
         ],
         compiler_params=params(),
         name=name,
-    )(src, dst, count, refresh, fx, delta, tiles)
+    )(src, dst, count, refresh, fx, mask, gh, source, tiles)
 
 
 def call_scatter(refresh, weight, own, gw, arr, picked):
@@ -874,11 +828,16 @@
 ):
     arr, fx, source = call_gather(features.T, weight, refresh, stale_cache)
     mask = train_mask.reshape(PER, TILE)
-    hidden, delta = call_forward(
-        tile_src, tile_dst, tile_count, mask, grad_hidden, source, adj_tiles
-    )
-    picked, own, gw = call_backward(
-        tile_src, tile_dst, tile_count, refresh, fx, delta, adj_tiles
+    hidden, picked, own, gw = call_tiles(
+        tile_src,
+        tile_dst,
+        tile_count,
+        refresh,
+        fx,
+        mask,
+        grad_hidden,
+        source,
+        adj_tiles,
     )
     grad_features, grad_weight = call_scatter(refresh, weight, own, gw, arr, picked)
     return hidden, grad_features.T, grad_weight

time: 123 us -> 111 us (0.902)
  Pallas kernels: 119 us -> 107 us
    pallas_call x1, Pallas kernels: 44.9 us -> 36 us  [call_gather(): pl.pallas_call(gather_kernel, out_shape=(shape((CLASS, REF, TILE), BF16),...]
    pallas_call x1, Pallas kernels: 48.1 us -> 43.4 us  [call_scatter(): pl.pallas_call(scatter_kernel, out_shape=(shape((64, ROWS), BF16), shape(...]
    pallas_call x2 -> x1, Pallas kernels: 25.6 us -> 27.2 us  [call_tiles(): pl.pallas_call(tiles_kernel, out_shape=(shape((ROWS, TILE), BF16), shape(...]
where the time goes in v5:
time: 111 us
  Pallas kernels  107 us (96%)
  local copies, waits for them, and re-layouts  3.04 us (3%)
  between operations  1.3 us (1%)
    pallas_call x1, Pallas kernels, call_scatter(): pl.pallas_call(scatter_kernel, out_shape=(shape((64, ROWS), BF16), shape(...  43.4 us
    pallas_call x1, Pallas kernels, call_gather(): pl.pallas_call(gather_kernel, out_shape=(shape((CLASS, REF, TILE), BF16),...  36 us
    pallas_call x1, Pallas kernels, call_tiles(): pl.pallas_call(tiles_kernel, out_shape=(shape((ROWS, TILE), BF16), shape(...  27.2 us
    unnamed x2, local copies, waits for them, and re-layouts  3.04 us

profile of v5, /device:TPU:0, one launch (start us, length us, event | category | flops | bytes accessed | tf_op | source)
XLA Modules:
  0.0 111.0 jit_solution(17271785877054216762)
XLA Ops:
  1.3 36.0 %gather_refreshed.1 = (bf16[32,256,128]{2,1,0:T(8,128)(2,1)}, bf16[128,1024]{1,0:T(8,128)(2,1)}, bf16[65536,128]{1,0:T(8,128)(2,1)}) custom-call(bf16[64,1024]{1,0:T(8,128)(2,1)} %bitcast.3, bf16[64,256]{1,0:T(8,128)(2,1)} %w_hbm.3, s32[64,256]{1,0:T(8,128)} %refresh_hbm.5, bf16[65536,128]{1,0:T(8,128)(2,1)} %stale_hbm.1), custom_call_target="tpu_custom_call" | custom-call | tf_op jit(solution)/shard_map/gather_refreshed/pallas_call | solution.py:717
  37.3 27.2 %tiles.1 = (bf16[1024,128]{1,0:T(8,128)(2,1)}, bf16[64,128,256]{2,1,0:T(8,128)(2,1)}, bf16[128,1024]{1,0:T(8,128)(2,1)}, f32[128,128]{1,0:T(8,128)}) custom-call(s32[768]{0:T(1024)} %src_ref.1, s32[768]{0:T(1024)} %dst_ref.1, s32[1]{0:T(128)S(6)} %copy.15.count_ref, s32[64,256]{1,0:T(8,128)} %refresh_hbm.5, bf16[128,1024]{1,0:T(8,128)(2,1)} %get-tuple-element.12.fx_hbm, ...), custom_call_target="tpu_custom_call" | custom-call | tf_op jit(solution)/shard_map/tiles/pallas_call | solution.py:752
  64.5 43.4 %scatter_gradients.1 = (bf16[64,1024]{1,0:T(8,128)(2,1)}, f32[64,256]{1,0:T(8,128)}) custom-call(s32[64,256]{1,0:T(8,128)} %refresh_hbm.5, bf16[64,256]{1,0:T(8,128)(2,1)} %w_hbm.3, bf16[128,1024]{1,0:T(8,128)(2,1)} %get-tuple-element.15.own_hbm, f32[128,128]{1,0:T(8,128)} %get-tuple-element.16.gw_hbm, bf16[32,256,128]{2,1,0:T(8,128)(2,1)} %get-tuple-element.17.arr_hbm, ...), custom_call_target="tpu_custom_call" | custom-call | tf_op jit(solution)/shard_map/scatter_gradients/pallas_call | solution.py:784
  107.9 1.6 %copy.16 = bf16[1024,64]{0,1:T(8,128)(2,1)} copy(bf16[1024,64]{0,1:T(8,128)(2,1)} %bitcast.4) | data formatting | bytes 262144
  109.5 1.5 %copy.17 = f32[64,256]{1,0:T(8,128)} copy(f32[64,256]{1,0:T(8,128)} %get-tuple-element.26) | data formatting | bytes 131072

commit v6 on v5

--- a/solution.py
+++ b/solution.py
@@ -38,6 +38,7 @@
         self.b = self.y * (1 - self.core) + self.x * self.core
         self.sibling = self.dom + 1 - 2 * self.core
         self.z_pair = self.dom + 2 - 4 * self.z
+        self.cross = self.sibling + 2 - 4 * self.z
         self.a_next = self.at(self.a + 1, self.b)
         self.a_prev = self.at(self.a + 3, self.b)
         self.b_next = self.at(self.a, self.b + 1)
@@ -63,7 +64,7 @@
         near = near + more
         for device in near:
             pl.semaphore_signal(barrier, inc=1, device_id=(device, self.feat), device_id_type=MESH)
-        pairs = (self.dom, self.z_pair) if cross else (self.dom,)
+        pairs = (self.dom, self.sibling, self.z_pair, self.cross) if cross else (self.dom,)
         for device in pairs:
             pl.semaphore_signal(
                 barrier, inc=1, device_id=(device, 1 - self.feat), device_id_type=MESH
@@ -86,8 +87,9 @@
 
 
 def refresh_by_rows(row):
-    rows = lax.broadcasted_iota(I32, (ROWS, REF), 0)
-    return (rows == row).astype(F32).astype(BF16)
+    rows = lax.broadcasted_iota(jnp.int16, (ROWS, REF), 0)
+    one, zero = jnp.ones((), BF16), jnp.zeros((), BF16)
+    return jnp.where(rows == row.astype(jnp.int16), one, zero)
 
 
 def fetch(sems, *pairs):
@@ -166,7 +168,6 @@
     w_copy = to_pair(1, weight.at[:, pair_columns], wcol.at[own_rows, :])
     w_copy.start()
     fx_copy = to_pair(2, fx.at[own_rows, :], fx.at[own_rows, :])
-    fx_copy.start()
 
     def shard(slot, target, kind, p):
         return pltpu.make_async_remote_copy(
@@ -284,6 +285,7 @@
     b0 = take_b(0)
     z_pair = take_plane(1)
     across = take_plane(6)
+    fx_copy.start()
     w_copy.wait_recv()
     lax.fori_loop(0, CLASS, wait_load, 0)
     merge(left, right, *b0)
@@ -503,9 +505,9 @@
     from_b2,
     from_a,
     from_z,
-    sum_core,
     sum_y,
     sum_x,
+    sum_out,
     sum_last,
     load_sem,
     small_sem,
@@ -513,7 +515,7 @@
     recv_sem,
 ):
     me = Place()
-    ready = me.greet(me.a_far, me.b_far, cross=True)
+    ready = me.greet(me.a_far, me.b_far, me.cross, cross=True)
     f, a, b, z = me.feat, me.a, me.b, me.z
     order = (2, 1, 3, 0)
 
@@ -579,6 +581,8 @@
         loads[h].wait()
         to_sib[h].wait_recv()
         add(first, 8, sib[pl.ds(first, 8)])
+
+    def launch(h):
         far, up, down = column(h, 2), column(h, 1), column(h, 3)
         b1.append(
             (
@@ -627,43 +631,60 @@
     def ring_sum(buffer, index, targets):
         return [send(buffer.at[index], buffer.at[index], target) for target in targets]
 
+    def total_of(terms):
+        one, two, three, four = [term.astype(F32) for term in terms]
+        return (one + two) + (three + four)
+
     def take_sum(buffer, copies):
         for copy in copies:
             copy.wait_recv()
-        return (buffer[0] + buffer[1]) + (buffer[2] + buffer[3])
+        return total_of([buffer[k] for k in range(RING)]).astype(BF16)
 
     fold(0)
+    launch(0)
     small[0].wait()
     small[1].wait()
     fold(1)
+    launch(1)
+    fold(2)
     weigh(0)
+    fold(3)
+    weigh(1)
+    weigh(2)
+    weigh(3)
+    sum_y[pl.ds(me.y, 1)] = jnp.transpose(gw[...]).astype(BF16)[None]
+    y_targets = [me.xy(me.x, me.y + k) for k in (1, 3, 2)]
+    y_copies = ring_sum(sum_y, me.y, y_targets)
+    launch(2)
     relay(0)
-    fold(2)
-    weigh(1)
+    launch(3)
     relay(1)
-    fold(3)
-    weigh(2)
     finish(0)
-    weigh(3)
-    sum_core[0] = jnp.transpose(gw[...])
-    core_copy = send(sum_core.at[0], sum_core.at[1], me.sibling)
     relay(2)
+    sum_x[pl.ds(me.x, 1)] = take_sum(sum_y, y_copies)[None]
+    x_targets = [me.xy(me.x + k, me.y) for k in (1, 3, 2)]
+    x_copies = ring_sum(sum_x, me.x, x_targets)
     finish(1)
     relay(3)
-    core_copy.wait_recv()
-    sum_y[pl.ds(me.y, 1)] = (sum_core[0] + sum_core[1])[None]
-    y_targets = [me.xy(me.x, me.y + k) for k in (1, 3, 2)]
-    y_copies = ring_sum(sum_y, me.y, y_targets)
-    finish(2)
     for copy in small[2:]:
         copy.wait()
     chosen = rows_by_refresh(refresh[pl.ds(me.dom, 1), :])
     own_columns, other_columns = column_block(f), column_block(1 - f)
+    own_rows, other_rows = half_rows(f), half_rows(1 - f)
     own_copy.wait_recv()
     base[...] = dot(weight[:, own_columns], own[...]) + dot(weight[:, other_columns], own_in[...])
-    sum_x[pl.ds(me.x, 1)] = take_sum(sum_y, y_copies)[None]
-    x_targets = [me.xy(me.x + k, me.y) for k in (1, 3, 2)]
-    x_copies = ring_sum(sum_x, me.x, x_targets)
+    finish(2)
+    sum_out[...] = take_sum(sum_x, x_copies)
+    place = me.core * 2 + z
+    sum_last[0, pl.ds(place, 1)] = sum_out[own_rows, :][None]
+    last_copies = [
+        send(sum_out.at[own_rows, :], sum_last.at[0, place], target)
+        for target in (me.sibling, me.z_pair, me.cross)
+    ]
+    last_copies += [
+        send(sum_out.at[other_rows, :], sum_last.at[1, place], target, 1 - f)
+        for target in (me.dom, me.sibling, me.z_pair, me.cross)
+    ]
     finish(3)
     here = column(3, 0)
     mine, theirs = work.at[pl.ds(here + z, 1)], work.at[pl.ds(here + 1 - z, 1)]
@@ -671,13 +692,6 @@
         send(theirs, from_z.at[pl.ds(0, 1)], me.z_pair),
         send(mine, from_z.at[pl.ds(1, 1)], me.dom, 1 - f),
         send(theirs, from_z.at[pl.ds(2, 1)], me.z_pair, 1 - f),
-    )
-    sum_last[0] = take_sum(sum_x, x_copies)
-    own_rows, other_rows = half_rows(f), half_rows(1 - f)
-    last_copies = (
-        send(sum_last.at[0, own_rows, :], sum_last.at[1, pl.ds(0, 64), :], me.z_pair),
-        send(sum_last.at[0, other_rows, :], sum_last.at[1, pl.ds(64, 64), :], me.dom, 1 - f),
-        send(sum_last.at[0, other_rows, :], sum_last.at[2, pl.ds(0, 64), :], me.z_pair, 1 - f),
     )
     for copy in z_copies:
         copy.wait_recv()
@@ -689,10 +703,15 @@
     gf_out[...] = (base[...] + dot(short.astype(BF16), chosen)).astype(BF16)
     for copy in last_copies:
         copy.wait_recv()
-    gw_out[:, own_columns] = sum_last[0, own_rows, :] + sum_last[1, pl.ds(0, 64), :]
-    gw_out[:, other_columns] = sum_last[1, pl.ds(64, 64), :] + sum_last[2, pl.ds(0, 64), :]
+    gw_out[:, own_columns] = total_of([sum_last[0, k] for k in range(4)])
+    gw_out[:, other_columns] = total_of([sum_last[1, k] for k in range(4)])
     for copy in sends:
         copy.wait_send()
+
+
+def finish_kernel(gf_hbm, gw_hbm, gf_out, gw_out, sems):
+    for copy in fetch(sems, (gf_hbm, gf_out), (gw_hbm, gw_out)):
+        copy.wait()
 
 
 VMEM = pl.BlockSpec(memory_space=pltpu.VMEM)
@@ -800,10 +819,10 @@
             scratch((RING, 2, 2, TILE, REF), BF16),
             scratch((3, 2, TILE, REF), BF16),
             scratch((3, TILE, REF), BF16),
-            scratch((2, TILE, TILE), F32),
-            scratch((RING, TILE, TILE), F32),
-            scratch((RING, TILE, TILE), F32),
-            scratch((3, TILE, TILE), F32),
+            scratch((RING, TILE, TILE), BF16),
+            scratch((RING, TILE, TILE), BF16),
+            scratch((TILE, TILE), BF16),
+            scratch((2, 4, 64, TILE), BF16),
             DMA((RING,)),
             DMA((5,)),
             DMA((48,)),
@@ -812,6 +831,18 @@
         compiler_params=params(collective_id=1, has_side_effects=True),
         name="scatter_gradients",
     )(refresh, weight, own, gw, arr, picked)
+
+
+def call_finish(gf, gw):
+    return pl.pallas_call(
+        finish_kernel,
+        out_shape=(shape(gf.shape, gf.dtype), shape(gw.shape, gw.dtype)),
+        in_specs=[ANY] * 2,
+        out_specs=(ANY, ANY),
+        scratch_shapes=[DMA((2,))],
+        compiler_params=params(),
+        name="finish",
+    )(gf, gw)
 
 
 def shards(
@@ -839,7 +870,8 @@
         source,
         adj_tiles,
     )
-    grad_features, grad_weight = call_scatter(refresh, weight, own, gw, arr, picked)
+    grads = call_scatter(refresh, weight, own, gw, arr, picked)
+    grad_features, grad_weight = call_finish(*grads)
     return hidden, grad_features.T, grad_weight
 
 

time: 111 us -> 110 us (level)
  local copies, waits for them, and re-layouts: 3.04 us -> 0 us
    pallas_call x0 -> x1, Pallas kernels: none -> 7.08 us  [call_finish(): pl.pallas_call(finish_kernel, out_shape=(shape(gf.shape, gf.dtype), shape...]
    pallas_call x1, Pallas kernels: 27.2 us -> 21.6 us  [call_tiles(): pl.pallas_call(tiles_kernel, out_shape=(shape((ROWS, TILE), BF16), shape(...]
    unnamed x2 -> x0, local copies, waits for them, and re-layouts: 3.04 us -> none
where the time goes in v6:
time: 110 us
  Pallas kernels  108 us (98%)
  between operations  1.46 us (1%)
    pallas_call x1, Pallas kernels, call_scatter(): pl.pallas_call(scatter_kernel, out_shape=(shape((64, ROWS), BF16), shape(...  44.1 us
    pallas_call x1, Pallas kernels, call_gather(): pl.pallas_call(gather_kernel, out_shape=(shape((CLASS, REF, TILE), BF16),...  35.7 us
    pallas_call x1, Pallas kernels, call_tiles(): pl.pallas_call(tiles_kernel, out_shape=(shape((ROWS, TILE), BF16), shape(...  21.6 us
    pallas_call x1, Pallas kernels, call_finish(): pl.pallas_call(finish_kernel, out_shape=(shape(gf.shape, gf.dtype), shape...  7.08 us

profile of v6, /device:TPU:0, one launch (start us, length us, event | category | flops | bytes accessed | tf_op | source)
XLA Modules:
  0.0 109.9 jit_solution(15805214391927518546)
XLA Ops:
  1.3 35.7 %gather_refreshed.1 = (bf16[32,256,128]{2,1,0:T(8,128)(2,1)}, bf16[128,1024]{1,0:T(8,128)(2,1)}, bf16[65536,128]{1,0:T(8,128)(2,1)}) custom-call(bf16[64,1024]{1,0:T(8,128)(2,1)} %bitcast.3, bf16[64,256]{1,0:T(8,128)(2,1)} %w_hbm.3, s32[64,256]{1,0:T(8,128)} %refresh_hbm.5, bf16[65536,128]{1,0:T(8,128)(2,1)} %stale_hbm.1), custom_call_target="tpu_custom_call" | custom-call | tf_op jit(solution)/shard_map/gather_refreshed/pallas_call | solution.py:736
  37.0 21.6 %tiles.1 = (bf16[1024,128]{1,0:T(8,128)(2,1)}, bf16[64,128,256]{2,1,0:T(8,128)(2,1)}, bf16[128,1024]{1,0:T(8,128)(2,1)}, f32[128,128]{1,0:T(8,128)}) custom-call(s32[768]{0:T(1024)} %src_ref.1, s32[768]{0:T(1024)} %dst_ref.1, s32[1]{0:T(128)S(6)} %copy.13.count_ref, s32[64,256]{1,0:T(8,128)} %refresh_hbm.5, bf16[128,1024]{1,0:T(8,128)(2,1)} %get-tuple-element.14.fx_hbm, ...), custom_call_target="tpu_custom_call" | custom-call | tf_op jit(solution)/shard_map/tiles/pallas_call | solution.py:771
  58.6 44.1 %scatter_gradients.1 = (bf16[64,1024]{1,0:T(8,128)(2,1)}, f32[64,256]{1,0:T(8,128)}) custom-call(s32[64,256]{1,0:T(8,128)} %refresh_hbm.5, bf16[64,256]{1,0:T(8,128)(2,1)} %w_hbm.3, bf16[128,1024]{1,0:T(8,128)(2,1)} %get-tuple-element.17.own_hbm, f32[128,128]{1,0:T(8,128)} %get-tuple-element.18.gw_hbm, bf16[32,256,128]{2,1,0:T(8,128)(2,1)} %get-tuple-element.19.arr_hbm, ...), custom_call_target="tpu_custom_call" | custom-call | tf_op jit(solution)/shard_map/scatter_gradients/pallas_call | solution.py:803
  102.6 7.1 %finish.1 = (bf16[64,1024]{1,0:T(8,128)(2,1)}, f32[64,256]{1,0:T(8,128)}) custom-call(bf16[64,1024]{1,0:T(8,128)(2,1)} %get-tuple-element.21.gf_hbm, f32[64,256]{1,0:T(8,128)} %get-tuple-element.22.gw_hbm), custom_call_target="tpu_custom_call" | custom-call | tf_op jit(solution)/shard_map/finish/pallas_call | solution.py:837

commit v7 on v6

--- a/solution.py
+++ b/solution.py
@@ -380,7 +380,6 @@
     live = count_ref[0]
     chunks = (live + CHUNK - 1) // CHUNK
     source_copy = pltpu.make_async_copy(source_hbm, source, source_sem)
-    source_copy.start()
 
     def tile_copy(turn):
         chunk = jnp.where(turn < chunks, turn, turn - chunks)
@@ -388,12 +387,8 @@
         part = pl.ds(chunk * CHUNK, CHUNK)
         return pltpu.make_async_copy(tiles_hbm.at[part], tiles.at[place], tile_sem.at[place])
 
-    for turn in range(TILE_RING):
-
-        @pl.when(turn < 2 * chunks)
-        def _():
-            tile_copy(turn).start()
-
+    tile_copy(0).start()
+    source_copy.start()
     loads = fetch(
         load_sem, (mask_hbm, mask), (gh_hbm, gh), (refresh_hbm, refresh), (fx_hbm, fx)
     )
@@ -405,6 +400,12 @@
 
     lax.fori_loop(0, BLOCKS // PER, clear, 0)
     acc[BLOCKS] = jnp.zeros((TILE, TILE), F32)
+    for turn in range(1, TILE_RING):
+
+        @pl.when(turn < 2 * chunks)
+        def _():
+            tile_copy(turn).start()
+
     source_copy.wait()
 
     def next_tiles(turn):
@@ -709,9 +710,9 @@
         copy.wait_send()
 
 
-def finish_kernel(gf_hbm, gw_hbm, gf_out, gw_out, sems):
-    for copy in fetch(sems, (gf_hbm, gf_out), (gw_hbm, gw_out)):
-        copy.wait()
+def finish_kernel(gf_ref, gw_ref, gf_out, gw_out):
+    gf_out[...] = gf_ref[...]
+    gw_out[...] = gw_ref[...]
 
 
 VMEM = pl.BlockSpec(memory_space=pltpu.VMEM)
@@ -837,9 +838,8 @@
     return pl.pallas_call(
         finish_kernel,
         out_shape=(shape(gf.shape, gf.dtype), shape(gw.shape, gw.dtype)),
-        in_specs=[ANY] * 2,
-        out_specs=(ANY, ANY),
-        scratch_shapes=[DMA((2,))],
+        in_specs=[VMEM] * 2,
+        out_specs=(VMEM, VMEM),
         compiler_params=params(),
         name="finish",
     )(gf, gw)

time: 110 us -> 103 us (0.936)
  Pallas kernels: 108 us -> 102 us
    pallas_call x1, Pallas kernels: 7.08 us -> 1.59 us  [call_finish(): pl.pallas_call(finish_kernel, out_shape=(shape(gf.shape, gf.dtype), shape...]
    pallas_call x1, Pallas kernels: 44.1 us -> 38.6 us  [call_scatter(): pl.pallas_call(scatter_kernel, out_shape=(shape((64, ROWS), BF16), shape(...]
    pallas_call x1, Pallas kernels: 21.6 us -> 26.1 us  [call_tiles(): pl.pallas_call(tiles_kernel, out_shape=(shape((ROWS, TILE), BF16), shape(...]
where the time goes in v7:
time: 103 us
  Pallas kernels  102 us (99%)
  between operations  1.3 us (1%)
    pallas_call x1, Pallas kernels, call_scatter(): pl.pallas_call(scatter_kernel, out_shape=(shape((64, ROWS), BF16), shape(...  38.6 us
    pallas_call x1, Pallas kernels, call_gather(): pl.pallas_call(gather_kernel, out_shape=(shape((CLASS, REF, TILE), BF16),...  35.7 us
    pallas_call x1, Pallas kernels, call_tiles(): pl.pallas_call(tiles_kernel, out_shape=(shape((ROWS, TILE), BF16), shape(...  26.1 us

profile of v7, /device:TPU:0, one launch (start us, length us, event | category | flops | bytes accessed | tf_op | source)
XLA Modules:
  0.0 103.2 jit_solution(16385301442402803004)
XLA Ops:
  1.3 35.7 %gather_refreshed.1 = (bf16[32,256,128]{2,1,0:T(8,128)(2,1)}, bf16[128,1024]{1,0:T(8,128)(2,1)}, bf16[65536,128]{1,0:T(8,128)(2,1)}) custom-call(bf16[64,1024]{1,0:T(8,128)(2,1)} %bitcast.3, bf16[64,256]{1,0:T(8,128)(2,1)} %w_hbm.3, s32[64,256]{1,0:T(8,128)} %refresh_hbm.5, bf16[65536,128]{1,0:T(8,128)(2,1)} %stale_hbm.1), custom_call_target="tpu_custom_call" | custom-call | tf_op jit(solution)/shard_map/gather_refreshed/pallas_call | solution.py:737
  37.0 26.1 %tiles.1 = (bf16[1024,128]{1,0:T(8,128)(2,1)}, bf16[64,128,256]{2,1,0:T(8,128)(2,1)}, bf16[128,1024]{1,0:T(8,128)(2,1)}, f32[128,128]{1,0:T(8,128)}) custom-call(s32[768]{0:T(1024)} %src_ref.1, s32[768]{0:T(1024)} %dst_ref.1, s32[1]{0:T(128)S(6)} %copy.13.count_ref, s32[64,256]{1,0:T(8,128)} %refresh_hbm.5, bf16[128,1024]{1,0:T(8,128)(2,1)} %get-tuple-element.14.fx_hbm, ...), custom_call_target="tpu_custom_call" | custom-call | tf_op jit(solution)/shard_map/tiles/pallas_call | solution.py:772
  63.0 38.6 %scatter_gradients.1 = (bf16[64,1024]{1,0:T(8,128)(2,1)}, f32[64,256]{1,0:T(8,128)}) custom-call(s32[64,256]{1,0:T(8,128)} %refresh_hbm.5, bf16[64,256]{1,0:T(8,128)(2,1)} %w_hbm.3, bf16[128,1024]{1,0:T(8,128)(2,1)} %get-tuple-element.17.own_hbm, f32[128,128]{1,0:T(8,128)} %get-tuple-element.18.gw_hbm, bf16[32,256,128]{2,1,0:T(8,128)(2,1)} %get-tuple-element.19.arr_hbm, ...), custom_call_target="tpu_custom_call" | custom-call | tf_op jit(solution)/shard_map/scatter_gradients/pallas_call | solution.py:804
  101.6 1.6 %finish.1 = (bf16[64,1024]{1,0:T(8,128)(2,1)}, f32[64,256]{1,0:T(8,128)}) custom-call(bf16[64,1024]{1,0:T(8,128)(2,1)} %get-tuple-element.21.gf_ref, f32[64,256]{1,0:T(8,128)} %get-tuple-element.22.gw_ref), custom_call_target="tpu_custom_call" | custom-call | tf_op jit(solution)/shard_map/finish/pallas_call | solution.py:838

commit v8 on v7

--- a/solution.py
+++ b/solution.py
@@ -277,19 +277,24 @@
         return carry
 
     def wait_load(k, carry):
-        load_rows(class_first + k).wait()
+        @pl.when(class_first + k != mine)
+        def _():
+            load_rows(class_first + k).wait()
+
         return carry
 
     lax.fori_loop(0, CLASS, start_load, 0)
+    w_copy.wait_recv()
+    load_rows(mine).wait()
+    merge(mine)
     left, right = take_plane(2), take_plane(3)
     b0 = take_b(0)
     z_pair = take_plane(1)
     across = take_plane(6)
     fx_copy.start()
-    w_copy.wait_recv()
     lax.fori_loop(0, CLASS, wait_load, 0)
     merge(left, right, *b0)
-    merge(z_pair, across, mine)
+    merge(z_pair, across)
     left, right = take_plane(4), take_plane(5)
     b2, b3 = take_b(2), take_b(3)
     merge(left, right, *b2)
@@ -342,7 +347,7 @@
 
 
 GROUP = 8
-CHUNK = 64
+CHUNK = 96
 TILE_RING = 3
 STAGED = 16
 
@@ -357,10 +362,13 @@
     gh_hbm,
     source_hbm,
     tiles_hbm,
-    hidden_ref,
+    hidden_hbm,
     picked_hbm,
-    own_ref,
-    gw_ref,
+    own_hbm,
+    gw_hbm,
+    hidden,
+    own,
+    gw,
     source,
     tiles,
     pre,
@@ -375,6 +383,7 @@
     tile_sem,
     load_sem,
     out_sem,
+    early_sem,
 ):
     me = lax.axis_index("dom")
     live = count_ref[0]
@@ -431,10 +440,13 @@
     for d in range(PER):
         total = pre[d]
         rows = pl.ds(d * TILE, TILE)
-        hidden_ref[rows, :] = jnp.maximum(total, 0.0).astype(BF16)
+        hidden[rows, :] = jnp.maximum(total, 0.0).astype(BF16)
         passed = jnp.where(total > 0, gh[rows, :].astype(F32), 0.0)
         kept = mask[pl.ds(d, 1), :].astype(F32)
         delta[d] = (jnp.transpose(passed) * kept).astype(BF16)
+
+    hidden_copy = pltpu.make_async_copy(hidden, hidden_hbm, early_sem.at[0])
+    hidden_copy.start()
 
     def backward(chunk, carry):
         turn = chunks + chunk
@@ -449,6 +461,15 @@
         return carry
 
     lax.fori_loop(0, chunks, backward, 0)
+    for k in range(PER):
+        own[:, pl.ds(k * TILE, TILE)] = acc[me * PER + k].astype(BF16)
+    gw[...] = lax.dot_general(
+        own[...], fx[...], (((1,), (1,)), ((), ())), preferred_element_type=F32
+    )
+    own_copy = pltpu.make_async_copy(own, own_hbm, early_sem.at[1])
+    own_copy.start()
+    gw_copy = pltpu.make_async_copy(gw, gw_hbm, early_sem.at[2])
+    gw_copy.start()
 
     def out_copy(slot):
         place = slot % STAGED
@@ -475,11 +496,9 @@
         return carry
 
     lax.fori_loop(0, PARTS // GROUP, pick, 0)
-    for k in range(PER):
-        own_ref[:, pl.ds(k * TILE, TILE)] = acc[me * PER + k].astype(BF16)
-    gw_ref[...] = lax.dot_general(
-        own_ref[...], fx[...], (((1,), (1,)), ((), ())), preferred_element_type=F32
-    )
+    hidden_copy.wait()
+    own_copy.wait()
+    gw_copy.wait()
     for slot in range(PARTS - STAGED, PARTS):
         out_copy(slot).wait()
 
@@ -667,13 +686,7 @@
     x_copies = ring_sum(sum_x, me.x, x_targets)
     finish(1)
     relay(3)
-    for copy in small[2:]:
-        copy.wait()
-    chosen = rows_by_refresh(refresh[pl.ds(me.dom, 1), :])
-    own_columns, other_columns = column_block(f), column_block(1 - f)
     own_rows, other_rows = half_rows(f), half_rows(1 - f)
-    own_copy.wait_recv()
-    base[...] = dot(weight[:, own_columns], own[...]) + dot(weight[:, other_columns], own_in[...])
     finish(2)
     sum_out[...] = take_sum(sum_x, x_copies)
     place = me.core * 2 + z
@@ -694,6 +707,16 @@
         send(mine, from_z.at[pl.ds(1, 1)], me.dom, 1 - f),
         send(theirs, from_z.at[pl.ds(2, 1)], me.z_pair, 1 - f),
     )
+    for copy in small[2:]:
+        copy.wait()
+    chosen = rows_by_refresh(refresh[pl.ds(me.dom, 1), :])
+    own_columns, other_columns = column_block(f), column_block(1 - f)
+    own_copy.wait_recv()
+    base[...] = dot(weight[:, own_columns], own[...]) + dot(weight[:, other_columns], own_in[...])
+    for copy in last_copies:
+        copy.wait_recv()
+    gw_out[:, own_columns] = total_of([sum_last[0, k] for k in range(4)])
+    gw_out[:, other_columns] = total_of([sum_last[1, k] for k in range(4)])
     for copy in z_copies:
         copy.wait_recv()
     carried = work[pl.ds(here + z, 1)][0].astype(F32) + from_z[0].astype(F32)
@@ -702,10 +725,6 @@
         weight[:, other_columns], carried_in.astype(BF16)
     )
     gf_out[...] = (base[...] + dot(short.astype(BF16), chosen)).astype(BF16)
-    for copy in last_copies:
-        copy.wait_recv()
-    gw_out[:, own_columns] = total_of([sum_last[0, k] for k in range(4)])
-    gw_out[:, other_columns] = total_of([sum_last[1, k] for k in range(4)])
     for copy in sends:
         copy.wait_send()
 
@@ -778,8 +797,11 @@
             shape((TILE, TILE), F32),
         ),
         in_specs=[SMEM] * 3 + [ANY] * 6,
-        out_specs=(VMEM, ANY, VMEM, VMEM),
+        out_specs=(ANY, ANY, ANY, ANY),
         scratch_shapes=[
+            scratch((ROWS, TILE), BF16),
+            scratch((TILE, ROWS), BF16),
+            scratch((TILE, TILE), F32),
             scratch((PARTS * ROWS, TILE), BF16),
             scratch((TILE_RING, CHUNK, TILE, TILE), BF16),
             scratch((PER + 1, TILE, TILE), F32),
@@ -794,6 +816,7 @@
             DMA((TILE_RING,)),
             DMA((4,)),
             DMA((STAGED,)),
+            DMA((3,)),
         ],
         compiler_params=params(),
         name=name,

time: 103 us -> 102 us (level)
  Pallas kernels: 102 us -> 100 us
    pallas_call x1, Pallas kernels: 26.1 us -> 20.5 us  [call_tiles(): pl.pallas_call(tiles_kernel, out_shape=(shape((ROWS, TILE), BF16), shape(...]
    pallas_call x1, Pallas kernels: 38.6 us -> 42.6 us  [call_scatter(): pl.pallas_call(scatter_kernel, out_shape=(shape((64, ROWS), BF16), shape(...]
where the time goes in v8:
time: 102 us
  Pallas kernels  100 us (98%)
  between operations  1.3 us (1%)
    pallas_call x1, Pallas kernels, call_scatter(): pl.pallas_call(scatter_kernel, out_shape=(shape((64, ROWS), BF16), shape(...  42.6 us
    pallas_call x1, Pallas kernels, call_gather(): pl.pallas_call(gather_kernel, out_shape=(shape((CLASS, REF, TILE), BF16),...  35.7 us
    pallas_call x1, Pallas kernels, call_tiles(): pl.pallas_call(tiles_kernel, out_shape=(shape((ROWS, TILE), BF16), shape(...  20.5 us

profile of v8, /device:TPU:0, one launch (start us, length us, event | category | flops | bytes accessed | tf_op | source)
XLA Modules:
  0.0 101.7 jit_solution(2172883560014526744)
XLA Ops:
  1.3 35.7 %gather_refreshed.1 = (bf16[32,256,128]{2,1,0:T(8,128)(2,1)}, bf16[128,1024]{1,0:T(8,128)(2,1)}, bf16[65536,128]{1,0:T(8,128)(2,1)}) custom-call(bf16[64,1024]{1,0:T(8,128)(2,1)} %bitcast.3, bf16[64,256]{1,0:T(8,128)(2,1)} %w_hbm.3, s32[64,256]{1,0:T(8,128)} %refresh_hbm.5, bf16[65536,128]{1,0:T(8,128)(2,1)} %stale_hbm.1), custom_call_target="tpu_custom_call" | custom-call | tf_op jit(solution)/shard_map/gather_refreshed/pallas_call | solution.py:756
  37.0 20.5 %tiles.1 = (bf16[1024,128]{1,0:T(8,128)(2,1)}, bf16[64,128,256]{2,1,0:T(8,128)(2,1)}, bf16[128,1024]{1,0:T(8,128)(2,1)}, f32[128,128]{1,0:T(8,128)}) custom-call(s32[768]{0:T(1024)} %src_ref.1, s32[768]{0:T(1024)} %dst_ref.1, s32[1]{0:T(128)S(6)} %copy.13.count_ref, s32[64,256]{1,0:T(8,128)} %refresh_hbm.5, bf16[128,1024]{1,0:T(8,128)(2,1)} %get-tuple-element.14.fx_hbm, ...), custom_call_target="tpu_custom_call" | custom-call | tf_op jit(solution)/shard_map/tiles/pallas_call | solution.py:791
  57.5 42.6 %scatter_gradients.1 = (bf16[64,1024]{1,0:T(8,128)(2,1)}, f32[64,256]{1,0:T(8,128)}) custom-call(s32[64,256]{1,0:T(8,128)} %refresh_hbm.5, bf16[64,256]{1,0:T(8,128)(2,1)} %w_hbm.3, bf16[128,1024]{1,0:T(8,128)(2,1)} %get-tuple-element.17.own_hbm, f32[128,128]{1,0:T(8,128)} %get-tuple-element.18.gw_hbm, bf16[32,256,128]{2,1,0:T(8,128)(2,1)} %get-tuple-element.19.arr_hbm, ...), custom_call_target="tpu_custom_call" | custom-call | tf_op jit(solution)/shard_map/scatter_gradients/pallas_call | solution.py:827
  100.1 1.6 %finish.1 = (bf16[64,1024]{1,0:T(8,128)(2,1)}, f32[64,256]{1,0:T(8,128)}) custom-call(bf16[64,1024]{1,0:T(8,128)(2,1)} %get-tuple-element.21.gf_ref, f32[64,256]{1,0:T(8,128)} %get-tuple-element.22.gw_ref), custom_call_target="tpu_custom_call" | custom-call | tf_op jit(solution)/shard_map/finish/pallas_call | solution.py:861
